TPU v7x, 512 devices: a whole 4x8x8 slice. The times are simulated.
512 devices in a mesh: leaf: 8 (over y), row: 8 (over z_hi, x), col: 8 (over z_lo, core).
Axes of the slice: x: 4, y: 8, z: 8 (z_hi: 2, z_lo: 4; z = z_hi * 4 + z_lo), core: 2. Of those that a mesh axis runs over, the one named last changes fastest.
Arguments:
- parent_front: float32 [2, 1, 8192, 8, 1024], P(None, None, ('leaf', 'row'), None, 'col'), as said below
- child_updates: float32 [2, 1, 8192, 4, 1024], P(None, None, ('leaf', 'row'), None, 'col')
- child_map: int32 [2, 32], replicated, may hold values from 0 to 63, as said below
Outputs:
- factored_front: float32 [2, 1, 8192, 8, 1024], P(None, None, ('leaf', 'row'), None, 'col')
Inputs may be any that keep to these rules, and one draw needn't show every extreme that they name: For each child c the entries child_map[c, :] are distinct, child_map[c, a] leaves the same remainder modulo 8 as a, and each child's map contains the first and the last parent block of every remainder class. Each row of the parent front's pivot block has a diagonal entry whose magnitude exceeds the norm of the row's other entries in that block; parent_front and child_updates are complex symmetric.
All inputs are finite; a program needn't handle non-finite values.
Results may differ from a plain program's by a relative error of at most 0.0015.
Values may be sent and summed in bfloat16 or wider, within the bound.
No kernel may reach another device: no remote copies, remote signals or barrier semaphores. Data moves between devices by JAX's collectives and lax.ppermute only.
A program may use at most 64 MiB of HBM per device.

v0:
```python
import jax
import jax.numpy as jnp
from jax import lax
from jax.sharding import PartitionSpec as P

NS_STEPS = 3


def spread(value, axis, source):
    kept = jnp.where(lax.axis_index(axis) == source, value, 0).astype(value.dtype)
    return lax.psum(kept, axis)


def complex_product(left, right):
    real_part = jnp.matmul(left[0], right[0], precision=lax.Precision.HIGHEST) - jnp.matmul(
        left[1], right[1], precision=lax.Precision.HIGHEST
    )
    imag_part = jnp.matmul(left[0], right[1], precision=lax.Precision.HIGHEST) + jnp.matmul(
        left[1], right[0], precision=lax.Precision.HIGHEST
    )
    return jnp.stack([real_part, imag_part])


def transposed_product(left, right):
    real_part = jnp.einsum(
        "rp,cp->rc", left[0], right[0], preferred_element_type=jnp.float32
    ) - jnp.einsum("rp,cp->rc", left[1], right[1], preferred_element_type=jnp.float32)
    imag_part = jnp.einsum(
        "rp,cp->rc", left[0], right[1], preferred_element_type=jnp.float32
    ) + jnp.einsum("rp,cp->rc", left[1], right[0], preferred_element_type=jnp.float32)
    return jnp.stack([real_part, imag_part])


def newton_inverse(pivot_block):
    diag_real = jnp.diagonal(pivot_block[0])
    diag_imag = jnp.diagonal(pivot_block[1])
    denominator = diag_real * diag_real + diag_imag * diag_imag
    current = jnp.stack([jnp.diag(diag_real / denominator), jnp.diag(-diag_imag / denominator)])
    for newton_step in range(NS_STEPS):
        product = complex_product(pivot_block, current)
        current = 2.0 * current - complex_product(current, product)
    return current


def local(parent_front, child_updates, child_map):
    leaf_count = lax.axis_size("leaf")
    row_count = lax.axis_size("row")
    col_count = lax.axis_size("col")
    rank_count = leaf_count * row_count
    half_ranks = rank_count // 2
    my_row = lax.axis_index("row")
    my_col = lax.axis_index("col")
    my_rank = lax.axis_index("leaf") * row_count + my_row
    row_blocks = parent_front.shape[1]
    block_size = parent_front.shape[2]
    local_cols = parent_front.shape[3]
    child_rows = child_updates.shape[1]
    child_cols = child_updates.shape[3]
    child_order = child_map.shape[1]
    panel_width = 2 * block_size
    flat_map = child_map.reshape(-1)
    pieces = lax.all_gather(child_updates[None], "leaf", axis=0, tiled=True)
    senders = pieces.shape[0]
    source_leaf = jnp.arange(senders, dtype=jnp.int32)
    source_rank = source_leaf * row_count + my_row
    source_child = source_rank // half_ranks
    source_slot = source_rank % half_ranks
    child_block = (
        jnp.arange(child_rows, dtype=jnp.int32)[None, :] * half_ranks + source_slot[:, None]
    )
    target_rows = jnp.take(flat_map, source_child[:, None] * child_order + child_block)
    local_index = jnp.arange(row_blocks, dtype=jnp.int32)
    row_select = (
        (target_rows[:, :, None] % rank_count == my_rank)
        & (target_rows[:, :, None] // rank_count == local_index[None, None, :])
    ).astype(jnp.float32)
    column_block = jnp.arange(child_cols, dtype=jnp.int32) * col_count + my_col
    target_cols = jnp.take(flat_map, source_child[:, None] * child_order + column_block[None, :])
    col_select = (
        target_cols[:, :, None] // col_count
        == jnp.arange(local_cols, dtype=jnp.int32)[None, None, :]
    ).astype(jnp.float32)
    added = jnp.einsum(
        "ntu,nztxby,nbs->zuxsy", row_select, pieces, col_select, precision=lax.Precision.HIGHEST
    )
    assembled = parent_front + added
    first_block = assembled[:, :, :, 0, :]
    columns = [spread(first_block, "col", owner) for owner in range(2)]
    panel_rows = jnp.concatenate(columns, axis=3)
    pivot_parts = [
        spread(panel_rows[:, 0].astype(jnp.bfloat16), ("leaf", "row"), owner).astype(jnp.float32)
        for owner in range(2)
    ]
    pivot_block = jnp.concatenate(pivot_parts, axis=1)
    inverse = newton_inverse(pivot_block)
    multipliers = complex_product(
        panel_rows.reshape(2, row_blocks * block_size, panel_width), inverse
    )
    compact = panel_rows.astype(jnp.bfloat16)
    gathered = lax.all_gather(compact, ("leaf", "row"), axis=2, tiled=True)
    gathered = gathered.reshape(
        2, row_blocks, rank_count // col_count, col_count, block_size, panel_width
    )
    gathered = lax.dynamic_index_in_dim(gathered, my_col, axis=3, keepdims=False)
    column_panel = gathered.reshape(2, local_cols * block_size, panel_width)
    update_all = transposed_product(multipliers.astype(jnp.bfloat16), column_panel)
    schur_part = assembled - update_all.reshape(assembled.shape)
    column_start = jnp.minimum(my_col, 1) * block_size
    mult_piece = lax.dynamic_slice_in_dim(multipliers, column_start, block_size, axis=2)
    mult_piece = mult_piece.reshape(2, row_blocks, block_size, 1, block_size)
    global_row = jnp.arange(row_blocks, dtype=jnp.int32) * rank_count + my_rank
    global_col = jnp.arange(local_cols, dtype=jnp.int32) * col_count + my_col
    pivot_row = (global_row < 2)[None, :, None, None, None]
    panel_col = (global_col < 2)[None, None, None, :, None]
    return jnp.where(pivot_row, assembled, jnp.where(panel_col, mult_piece, schur_part))


def solution(mesh):
    in_specs = (
        P(None, None, ("leaf", "row"), None, "col"),
        P(None, None, ("leaf", "row"), None, "col"),
        P(),
    )
    out_specs = P(None, None, ("leaf", "row"), None, "col")
    return jax.shard_map(local, mesh=mesh, in_specs=in_specs, out_specs=out_specs, check_vma=False)
```

profile of v0, /device:TPU:2, one launch (start us, length us, event | category | flops | bytes accessed | tf_op | source)
XLA Modules:
  0.0 1166.9 jit_solution(15491226585552927433)
XLA Ops:
  6.5 2.0 copy.17
  8.8 0.8 reshape.505
  9.6 0.7 gather_fusion
  10.5 0.7 gather_fusion.1
  11.2 60.0 %all-gather.6.cloned.1.call-done = f32[16,1,128,4,128]{4,2,3,1,0:T(8,128)} async-done(((f32[2,1,128,4,128]{4,2,3,1,0:T(8,128)}), f32[16,1,128,4,128]{4,2,3,1,0:T(8,128)}) %all-gather.6.cloned.1.call-update) | async-done | bytes 4194320 | tf_op jit(solution)/shard_map/all_gather | solution.py:62
  71.2 11.3 fusion.5
  82.6 0.8 broadcast_select_fusion
  83.4 0.7 select_bitcast_fusion.2
  84.1 75.9 %all-reduce.5.cloned.1.call-done = (f32[2,1,128,128]{3,2,0,1:T(8,128)}, f32[2,1,128,128]{3,2,0,1:T(8,128)}) async-done(((f32[2,1,128,128]{3,2,0,1:T(8,128)}, f32[2,1,128,128]{3,2,0,1:T(8,128)}), (f32[2,1,128,128]{3,2,0,1:T(8,128)}, f32[2,1,128,128]{3,2,0,1:T(8,128)})) %all-reduce.5.cloned.1.call-update) | async-done | bytes 262160 | tf_op jit(solution)/shard_map/psum | solution.py:11
  160.0 0.9 constant_dynamic-update-slice_fusion.1
  161.0 0.9 constant_dynamic-update-slice_fusion
  161.9 0.7 select_bitcast_fusion
  162.6 0.7 select_bitcast_fusion.1
  163.9 785.1 %all-reduce.7.cloned.1.call-done = (bf16[2,128,256]{2,1,0:T(8,128)(2,1)}, bf16[2,128,256]{2,1,0:T(8,128)(2,1)}) async-done(((bf16[2,128,256]{2,1,0:T(8,128)(2,1)}, bf16[2,128,256]{2,1,0:T(8,128)(2,1)}), (bf16[2,128,256]{2,1,0:T(8,128)(2,1)}, bf16[2,128,256]{2,1,0:T(8,128)(2,1)})) %all-reduce.7.cloned.1.call-update) | async-done | bytes 262160 | tf_op jit(solution)/shard_map/psum | solution.py:11
  949.0 0.9 constant_dynamic-update-slice_fusion.3
  949.9 0.9 constant_dynamic-update-slice_fusion.2
  951.0 2.3 gather_fusion.2
  953.3 2.3 gather_fusion.3
  956.7 0.4 fusion.30
  957.5 0.4 fusion.15
  957.9 0.4 fusion.27
  958.4 0.4 fusion.14
  960.7 0.4 fusion.13
  961.1 0.4 fusion.39
  961.5 0.4 fusion.12
  962.9 0.4 fusion.44
  963.6 0.4 fusion.11
  964.0 0.4 fusion.43
  964.4 0.4 fusion.10
  966.1 190.3 %all-gather.4.cloned.1.call-done = bf16[2,1,8192,256]{3,2,0,1:T(8,128)(2,1)} async-done(((bf16[2,1,128,256]{3,2,0,1:T(8,128)(2,1)}), bf16[2,1,8192,256]{3,2,0,1:T(8,128)(2,1)}) %all-gather.4.cloned.1.call-update) | async-done | bytes 8388624 | tf_op jit(solution)/shard_map/all_gather | solution.py:100
  1156.4 1.3 constant_dynamic-slice_fusion
  1159.1 1.2 fusion.20
  (58 shorter events, 8.6 us)
Async XLA Ops:
  6.5 64.7 %copy-start.1 = (f32[2,1,128,8,128]{4,3,2,1,0:T(8,128)S(1)}, f32[2,1,128,8,128]{4,3,2,1,0:T(8,128)}, u32[]{:S(2)}) copy-start(f32[2,1,128,8,128]{4,3,2,1,0:T(8,128)} %param.3) | copy-start | bytes 3145732
  6.5 64.7 %all-gather.6.cloned.1.call-start = ((), (), s32[]{:S(2)}) async-start(), calls=%async_computation.1 | async-start | bytes 4718592 | tf_op jit(solution)/shard_map/all_gather | solution.py:62
  8.5 151.5 %all-reduce.5.cloned.1.call-start = ((), (), s32[]{:S(2)}) async-start(), calls=%async_computation.2 | async-start | bytes 524288 | tf_op jit(solution)/shard_map/psum | solution.py:11
  84.1 864.9 %all-reduce.7.cloned.1.call-start = ((), (), s32[]{:S(2)}) async-start(), calls=%async_computation.3 | async-start | bytes 524288 | tf_op jit(solution)/shard_map/psum | solution.py:11
  162.5 1.0 copy-start
  163.3 993.1 %all-gather.4.cloned.1.call-start = ((), (), s32[]{:S(2)}) async-start(), calls=%async_computation | async-start | bytes 8519680 | tf_op jit(solution)/shard_map/all_gather | solution.py:100
Sparse Core Ops, SparseCore 0:
  9.4 61.7 all-gather.5
  84.2 75.7 all-reduce.4
  163.4 785.5 all-reduce.6
  953.3 203.0 all-gather.3
where the time goes:
time: 1170 us
  waiting for transfers between devices  1110 us (95%)
  matrix products  22.2 us (2%)
  local copies, waits for them, and re-layouts  14.2 us (1%)
  between operations  13.6 us (1%)
    psum x2, waiting for transfers between devices, spread(): return lax.psum(kept, axis)  861 us
    all_gather x1, waiting for transfers between devices, local(): gathered = lax.all_gather(compact, ('leaf', 'row'), axis=2, tiled=True)  190 us
    all_gather x1, waiting for transfers between devices, local(): pieces = lax.all_gather(child_updates[None], 'leaf', axis=0, tiled=True)  60 us
  transfers between devices with their start and end apart: 4, of which 4 were waited for; matrix products, arithmetic and copies ran while one was open for 2% of the time, Pallas kernels for 0%

commit v1 on v0

v1 whole, which is shorter than its diff:
```python
import jax
import jax.numpy as jnp
from jax import lax
from jax.experimental import pallas as pl
from jax.experimental.pallas import tpu as pltpu
from jax.sharding import PartitionSpec as P

BLK = 128
SLOTS = 8
CHILD_SLOTS = 4
RANKS = 8
SLICE = BLK // RANKS
F32 = jnp.float32
BF16 = jnp.bfloat16
VMEM_LIMIT = 40 * 1024 * 1024


def vmem():
    return pl.BlockSpec(memory_space=pltpu.VMEM)


def smem():
    return pl.BlockSpec(memory_space=pltpu.SMEM)


def params():
    return pltpu.CompilerParams(vmem_limit_bytes=VMEM_LIMIT)


def top_rows_kernel(map_ref, front_ref, child_ref, out_ref, acc_ref):
    leaf, row, col = (lax.axis_index(name) for name in ("leaf", "row", "col"))
    child = leaf // CHILD_SLOTS
    hit = map_ref[child, (leaf % CHILD_SLOTS) * RANKS + row] == row

    @pl.when(leaf == 0)
    def _():
        for z in range(2):
            for j in range(SLOTS):
                acc_ref[j, z] = front_ref[z, pl.ds(j, BLK, stride=SLOTS), :]

    @pl.when(leaf != 0)
    def _():
        acc_ref[...] = jnp.zeros_like(acc_ref)

    @pl.when(hit)
    def _():
        for k in range(CHILD_SLOTS):
            slot = map_ref[child, k * RANKS + col] // RANKS
            for z in range(2):
                acc_ref[slot, z] += child_ref[z, pl.ds(k, BLK, stride=CHILD_SLOTS), :]

    for d in range(SLOTS):
        for z in range(2):
            out_ref[d, z, :BLK, :] = acc_ref[d, z].astype(BF16)
            out_ref[d, z, BLK:, :] = acc_ref[0, z, d * SLICE : (d + 1) * SLICE, :].astype(BF16)


def top_rows(child_map, front, child):
    return pl.pallas_call(
        top_rows_kernel,
        out_shape=jax.ShapeDtypeStruct((SLOTS, 2, BLK + SLICE, BLK), BF16),
        in_specs=[smem(), vmem(), vmem()],
        out_specs=vmem(),
        scratch_shapes=[pltpu.VMEM((SLOTS, 2, BLK, BLK), F32)],
        compiler_params=params(),
        name="top_rows",
    )(child_map, front, child)


def assemble_kernel(map_ref, front_ref, pieces_ref, out_ref, piece_ref, sem):
    leaf, row, col = (lax.axis_index(name) for name in ("leaf", "row", "col"))
    out_ref[...] = front_ref[...]
    for child in range(2):
        for source in range(CHILD_SLOTS):
            @pl.when(map_ref[child, source * RANKS + row] // RANKS == leaf)
            def _():
                copy = pltpu.make_async_copy(
                    pieces_ref.at[child * CHILD_SLOTS + source], piece_ref, sem
                )
                copy.start()
                copy.wait()
                for k in range(CHILD_SLOTS):
                    slot = map_ref[child, k * RANKS + col] // RANKS
                    for z in range(2):
                        where = pl.ds(slot, BLK, stride=SLOTS)
                        out_ref[z, where, :] += piece_ref[z, pl.ds(k, BLK, stride=CHILD_SLOTS), :]


def assemble(child_map, front, pieces):
    return pl.pallas_call(
        assemble_kernel,
        out_shape=jax.ShapeDtypeStruct(front.shape, F32),
        in_specs=[smem(), vmem(), pl.BlockSpec(memory_space=pl.ANY)],
        out_specs=vmem(),
        scratch_shapes=[pltpu.VMEM(pieces.shape[1:], F32), pltpu.SemaphoreType.DMA],
        compiler_params=params(),
        cost_estimate=pl.CostEstimate(flops=1 << 20, bytes_accessed=3 << 20, transcendentals=0),
        name="assemble",
    )(child_map, front, pieces)


def split(x):
    high = x.astype(BF16)
    return high, (x - high.astype(F32)).astype(BF16)


def dot(a, b):
    return jnp.dot(a, b, preferred_element_type=F32)


def product(left, right):
    ls = [split(x) for x in left]
    rs = [split(x) for x in right]

    def real(a, b):
        return dot(a[0], b[0]) + (dot(a[0], b[1]) + dot(a[1], b[0]))

    return (
        real(ls[0], rs[0]) - real(ls[1], rs[1]),
        real(ls[0], rs[1]) + real(ls[1], rs[0]),
    )


def multipliers_kernel(pieces_ref, rows_ref, left_ref, mult_ref, a_ref):
    width = 2 * BLK
    for d in range(RANKS):
        for h in range(2):
            for z in range(2):
                for g in range(2):
                    a_ref[
                        z, h * BLK + d * SLICE : h * BLK + (d + 1) * SLICE, g * BLK : (g + 1) * BLK
                    ] = pieces_ref[d, h, z, g * SLICE : (g + 1) * SLICE, :].astype(F32)
    a_re, a_im = a_ref[0], a_ref[1]
    diagonal = lax.broadcasted_iota(jnp.int32, (width, width), 0) == lax.broadcasted_iota(
        jnp.int32, (width, width), 1
    )
    d_re = jnp.sum(jnp.where(diagonal, a_re, 0.0), axis=1, keepdims=True)
    d_im = jnp.sum(jnp.where(diagonal, a_im, 0.0), axis=1, keepdims=True)
    size = d_re * d_re + d_im * d_im
    x_re, x_im = d_re / size, -d_im / size
    e_re = jnp.where(diagonal, 0.0, -(x_re * a_re - x_im * a_im))
    e_im = jnp.where(diagonal, 0.0, -(x_re * a_im + x_im * a_re))
    e0 = (e_re, e_im)
    e1 = product(e0, e0)
    e2 = product(e1, e1)
    r_re, r_im = rows_ref[0].astype(F32), rows_ref[1].astype(F32)
    t = (x_re * r_re - x_im * r_im, x_re * r_im + x_im * r_re)
    for e in (e0, e1, e2):
        step = product(e, t)
        t = (t[0] + step[0], t[1] + step[1])
    w_re, w_im = t[0].T, t[1].T
    mult_ref[0] = w_re
    mult_ref[1] = w_im
    left_ref[:BLK, :width] = w_re.astype(BF16)
    left_ref[:BLK, width:] = (-w_im).astype(BF16)
    left_ref[BLK:, :width] = w_im.astype(BF16)
    left_ref[BLK:, width:] = w_re.astype(BF16)


def multipliers(pieces, rows):
    width = 2 * BLK
    return pl.pallas_call(
        multipliers_kernel,
        out_shape=(
            jax.ShapeDtypeStruct((width, 2 * width), BF16),
            jax.ShapeDtypeStruct((2, BLK, width), F32),
        ),
        in_specs=[vmem(), vmem()],
        out_specs=(vmem(), vmem()),
        scratch_shapes=[pltpu.VMEM((2, width, width), F32)],
        compiler_params=params(),
        cost_estimate=pl.CostEstimate(flops=3 << 30, bytes_accessed=1 << 20, transcendentals=0),
        name="multipliers",
    )(pieces, rows)


def update_kernel(left_ref, mult_ref, panel_ref, front_ref, out_ref):
    leaf, row, col = (lax.axis_index(name) for name in ("leaf", "row", "col"))
    is_pivot_row = (leaf == 0) & (row < 2)

    @pl.when(is_pivot_row)
    def _():
        out_ref[...] = front_ref[...]

    @pl.when(jnp.logical_not(is_pivot_row))
    def _():
        left = left_ref[...]
        for j in range(SLOTS):
            update = dot(left, panel_ref[j])
            where = pl.ds(j, BLK, stride=SLOTS)
            for z in range(2):
                out_ref[z, where, :] = front_ref[z, where, :] - update[z * BLK : (z + 1) * BLK]
        for g in range(2):
            @pl.when(col == g)
            def _():
                for z in range(2):
                    out_ref[z, pl.ds(0, BLK, stride=SLOTS), :] = mult_ref[z, :, g * BLK : (g + 1) * BLK]


def update(left, mult, panel, front):
    return pl.pallas_call(
        update_kernel,
        out_shape=jax.ShapeDtypeStruct(front.shape, F32),
        in_specs=[vmem()] * 4,
        out_specs=vmem(),
        compiler_params=params(),
        name="update",
    )(left, mult, panel, front)


def exchange(x, axis):
    return lax.all_to_all(x, axis, 0, 0)


def spread(x, axis):
    return exchange(jnp.broadcast_to(x[None], (RANKS,) + x.shape), axis)


def local(parent_front, child_updates, child_map):
    front = parent_front.reshape(2, BLK * SLOTS, BLK)
    child = child_updates.reshape(2, BLK * CHILD_SLOTS, BLK)
    pieces = lax.all_gather(child, "leaf", axis=0, tiled=False)
    parts = exchange(top_rows(child_map, front, child), "leaf")
    top = jnp.sum(parts.astype(F32), axis=0).astype(BF16)
    pivot = spread(top[:, BLK:], "col")
    both = spread(jnp.concatenate([top[:, :BLK], pivot[0], pivot[1]], axis=1), "row")
    own = jnp.concatenate([both[0, :, :BLK], both[1, :, :BLK]], axis=1)
    panel = lax.all_gather(own, "leaf", axis=0, tiled=False)
    swap = [(a * RANKS + b, b * RANKS + a) for a in range(RANKS) for b in range(RANKS)]
    rows = lax.ppermute(own, ("row", "col"), swap)
    pivot_pieces = spread(both[:2, :, BLK:], "leaf")
    left, mult = multipliers(pivot_pieces, rows)
    assembled = assemble(child_map, front, pieces)
    result = update(left, mult, panel.reshape(SLOTS, 4 * BLK, BLK), assembled)
    return result.reshape(parent_front.shape)


def solution(mesh):
    spec = P(None, None, ("leaf", "row"), None, "col")
    return jax.shard_map(
        local, mesh=mesh, in_specs=(spec, spec, P()), out_specs=spec, check_vma=False
    )
```

time: 1170 us -> 131 us (0.11)
  the two profiles are of different devices: /device:TPU:2 before, /device:TPU:72 now
where the time goes in v1:
time: 131 us; the launch traced here: 130 us
  blocking collectives  60.8 us (46%)
  waiting for transfers between devices  25.9 us (20%)
  starting transfers between devices  14.9 us (11%)
  between operations  13.5 us (10%)
  local copies, waits for them, and re-layouts  7.87 us (6%)
  Pallas kernels  6.32 us (5%)
    all_to_all x2, blocking collectives, exchange(): return lax.all_to_all(x, axis, 0, 0)  60.8 us
    all_to_all x2, starting transfers between devices, exchange(): return lax.all_to_all(x, axis, 0, 0)  12.9 us
    all_gather x1, waiting for transfers between devices, local(): panel = lax.all_gather(own, 'leaf', axis=0, tiled=False)  9.43 us
    ppermute x1, waiting for transfers between devices, local(): rows = lax.ppermute(own, ('row', 'col'), swap)  8.1 us
    all_to_all x2, waiting for transfers between devices, exchange(): return lax.all_to_all(x, axis, 0, 0)  7.63 us
    unnamed x14, local copies, waits for them, and re-layouts  6.36 us
    pallas_call x1, Pallas kernels, multipliers(): pl.pallas_call(multipliers_kernel, out_shape=(jax.ShapeDtypeStruct((width...  2.99 us
  transfers between devices with their start and end apart: 5, of which 4 were waited for; matrix products, arithmetic and copies ran while one was open for 2% of the time, Pallas kernels for 4%

profile of v1, /device:TPU:72, one launch (start us, length us, event | category | flops | bytes accessed | tf_op | source)
XLA Modules:
  0.0 130.1 jit_solution(14490063957867026402)
XLA Ops:
  6.5 0.0 all-gather.4.cloned.1.call-start
  6.5 0.7 all-gather.4.cloned.1.call-update
  7.3 0.0 copy-start.1
  7.3 1.2 copy-done.1
  8.5 1.0 copy-done.3
  9.5 0.7 copy-done.5
  10.2 0.7 top_rows.1
  10.9 27.4 %all_to_all.20 = bf16[8,2,144,128]{3,2,1,0:T(8,128)(2,1)S(1)} all-to-all(bf16[8,2,144,128]{3,2,1,0:T(8,128)(2,1)S(1)} %top_rows.1), channel_id=1, replica_groups=mesh['leaf'=8,'row'=8,'col'=8] {'leaf'}, dimensions={0} | all-to-all | bytes 1179648 | tf_op jit(solution)/shard_map/all_to_all | solution.py:212
  38.3 0.1 reduce_sum.12
  38.4 0.6 broadcast_in_dim.6
  39.1 7.2 %all-to-all-start.1 = ((bf16[8,2,16,128]{3,2,1,0:T(8,128)(2,1)}), bf16[8,2,16,128]{3,2,1,0:T(8,128)(2,1)S(1)}, u32[]{:S(2)}, u32[]{:S(2)}) async-start(bf16[8,2,16,128]{3,2,1,0:T(8,128)(2,1)} %broadcast_in_dim.6), calls=%async_computation.1 | async-start | bytes 131072 | tf_op jit(solution)/shard_map/all_to_all | solution.py:212
  46.3 0.0 all-gather.6.cloned.1.call-start
  46.3 4.6 %all-to-all-done.1 = bf16[8,2,16,128]{3,2,1,0:T(8,128)(2,1)S(1)} async-done(((bf16[8,2,16,128]{3,2,1,0:T(8,128)(2,1)}), bf16[8,2,16,128]{3,2,1,0:T(8,128)(2,1)S(1)}, u32[]{:S(2)}, u32[]{:S(2)}) %all-to-all-start.1) | async-done | bytes 65568 | tf_op jit(solution)/shard_map/all_to_all | solution.py:212
  51.0 0.1 broadcast_in_dim.7
  51.1 33.4 %all_to_all.21 = bf16[8,2,160,128]{3,2,1,0:T(8,128)(2,1)S(1)} all-to-all(bf16[8,2,160,128]{3,2,1,0:T(8,128)(2,1)S(1)} %broadcast_in_dim.7), channel_id=1, replica_groups=mesh['leaf'=8,'row'=8,'col'=8] {'row'}, dimensions={0} | all-to-all | bytes 1310720 | tf_op jit(solution)/shard_map/all_to_all | solution.py:212
  84.5 0.7 pad_maximum_fusion
  85.1 0.0 all-gather.6.cloned.1.call-update
  85.2 0.8 broadcast_in_dim.8
  85.9 5.7 %all-to-all-start.3 = ((bf16[8,2,2,32,128]{4,3,2,1,0:T(8,128)(2,1)}), bf16[8,2,2,32,128]{4,3,2,1,0:T(8,128)(2,1)S(1)}, u32[]{:S(2)}, u32[]{:S(2)}) async-start(bf16[8,2,2,32,128]{4,3,2,1,0:T(8,128)(2,1)} %broadcast_in_dim.8), calls=%async_computation.3 | async-start | bytes 524288 | tf_op jit(solution)/shard_map/all_to_all | solution.py:212
  91.6 2.0 %collective-permute-start = (bf16[2,256,128]{2,1,0:T(8,128)(2,1)}, bf16[2,256,128]{2,1,0:T(8,128)(2,1)S(1)}, u32[]{:S(2)}, u32[]{:S(2)}) collective-permute-start(bf16[2,256,128]{2,1,0:T(8,128)(2,1)} %pad_maximum_fusion), channel_id=1, source_target_pairs={{0,0},{1,8},{2,16},{3,24},{4,32},{5,40},{6,48},{7,56},{8,1},{9,9},... | collective-permute-start | bytes 393224 | tf_op jit(solution)/shard_map/ppermute | solution.py:230
  93.7 8.1 %collective-permute-done.rows_ref = bf16[2,256,128]{2,1,0:T(8,128)(2,1)S(1)} collective-permute-done((bf16[2,256,128]{2,1,0:T(8,128)(2,1)}, bf16[2,256,128]{2,1,0:T(8,128)(2,1)S(1)}, u32[]{:S(2)}, u32[]{:S(2)}) %collective-permute-start) | collective-permute-done | bytes 131104 | tf_op jit(solution)/shard_map/ppermute | solution.py:230
  101.8 3.0 %all-to-all-done.3.pieces_ref = bf16[8,2,2,32,128]{4,3,2,1,0:T(8,128)(2,1)S(1)} async-done(((bf16[8,2,2,32,128]{4,3,2,1,0:T(8,128)(2,1)}), bf16[8,2,2,32,128]{4,3,2,1,0:T(8,128)(2,1)S(1)}, u32[]{:S(2)}, u32[]{:S(2)}) %all-to-all-start.3) | async-done | bytes 262176 | tf_op jit(solution)/shard_map/all_to_all | solution.py:212
  104.8 3.0 %multipliers.1 = (bf16[256,512]{1,0:T(8,128)(2,1)S(1)}, f32[2,128,256]{2,1,0:T(8,128)S(1)}) custom-call(bf16[8,2,2,32,128]{4,3,2,1,0:T(8,128)(2,1)S(1)} %all-to-all-done.3.pieces_ref, bf16[2,256,128]{2,1,0:T(8,128)(2,1)S(1)} %collective-permute-done.rows_ref), custom_call_target="tpu_custom_call" | custom-call | flops 3221225472 | bytes 1048576 | tf_op jit(solution)/shard_map/multipliers/pallas_call | solution.py:162
  107.8 0.0 all-gather.4.cloned.1.call-done.pieces_ref
  107.8 0.0 copy-done.2
  107.8 0.0 copy-done.6
  107.8 0.0 copy-start
  107.8 2.2 %copy-done = f32[8,2,512,128]{3,2,1,0:T(8,128)S(1)} copy-done((f32[8,2,512,128]{3,2,1,0:T(8,128)S(1)}, f32[8,2,512,128]{3,2,1,0:T(8,128)}, u32[]{:S(2)}) %copy-start) | copy-done | bytes 4194328
  110.0 1.0 assemble.1.front_ref
  111.0 9.4 %all-gather.6.cloned.1.call-done = bf16[16,256,128]{2,1,0:T(8,128)(2,1)} async-done(((bf16[2,256,128]{2,1,0:T(8,128)(2,1)}), bf16[16,256,128]{2,1,0:T(8,128)(2,1)}) %all-gather.6.cloned.1.call-update) | async-done | bytes 1048592 | tf_op jit(solution)/shard_map/all_gather | solution.py:228
  120.4 1.2 copy-done.4
  121.6 1.7 %update.1 = f32[2,1024,128]{2,1,0:T(8,128)} custom-call(bf16[256,512]{1,0:T(8,128)(2,1)S(1)} %get-tuple-element.7.left_ref, f32[2,128,256]{2,1,0:T(8,128)S(1)} %get-tuple-element.8.mult_ref, bf16[8,512,128]{2,1,0:T(8,128)(2,1)S(1)} %bitcast.19, f32[2,1024,128]{2,1,0:T(8,128)S(1)} %assemble.1.front_ref), custom_call_target="tpu_custom_call" | custom-call | tf_op jit(solution)/shard_map/update/pallas_call | solution.py:201
  (11 shorter events, 0.0 us)
Async XLA Ops:
  6.5 101.2 %all-gather.4.cloned.1.call-start = ((), (), s32[]{:S(2)}) async-start(), calls=%async_computation.4 | async-start | bytes 4718592 | tf_op jit(solution)/shard_map/all_gather | solution.py:222
  7.3 1.2 copy-start.1
  8.5 1.0 copy-start.3
  9.5 0.7 copy-start.5
  39.1 11.9 %all-to-all-start.1 = ((bf16[8,2,16,128]{3,2,1,0:T(8,128)(2,1)}), bf16[8,2,16,128]{3,2,1,0:T(8,128)(2,1)S(1)}, u32[]{:S(2)}, u32[]{:S(2)}) async-start(bf16[8,2,16,128]{3,2,1,0:T(8,128)(2,1)} %broadcast_in_dim.6), calls=%async_computation.1 | async-start | bytes 131072 | tf_op jit(solution)/shard_map/all_to_all | solution.py:212
  46.3 74.1 %all-gather.6.cloned.1.call-start = ((), (), s32[]{:S(2)}) async-start(), calls=%async_computation.5 | async-start | bytes 1179648 | tf_op jit(solution)/shard_map/all_gather | solution.py:228
  85.9 18.8 %all-to-all-start.3 = ((bf16[8,2,2,32,128]{4,3,2,1,0:T(8,128)(2,1)}), bf16[8,2,2,32,128]{4,3,2,1,0:T(8,128)(2,1)S(1)}, u32[]{:S(2)}, u32[]{:S(2)}) async-start(bf16[8,2,2,32,128]{4,3,2,1,0:T(8,128)(2,1)} %broadcast_in_dim.8), calls=%async_computation.3 | async-start | bytes 524288 | tf_op jit(solution)/shard_map/all_to_all | solution.py:212
  91.6 16.2 %copy-start.2 = (f32[2,1,128,8,128]{4,3,2,1,0:T(8,128)S(1)}, f32[2,1,128,8,128]{4,3,2,1,0:T(8,128)}, u32[]{:S(2)}) copy-start(f32[2,1,128,8,128]{4,3,2,1,0:T(8,128)} %param.3) | copy-start | bytes 3145732
  91.6 16.2 %copy-start.6 = (s32[2,32]{1,0:T(2,128)S(1)}, s32[2,32]{1,0:T(2,128)}, u32[]{:S(2)}) copy-start(s32[2,32]{1,0:T(2,128)} %map_ref.3) | copy-start | bytes 772
  91.6 10.1 %collective-permute-start = (bf16[2,256,128]{2,1,0:T(8,128)(2,1)}, bf16[2,256,128]{2,1,0:T(8,128)(2,1)S(1)}, u32[]{:S(2)}, u32[]{:S(2)}) collective-permute-start(bf16[2,256,128]{2,1,0:T(8,128)(2,1)} %pad_maximum_fusion), channel_id=1, source_target_pairs={{0,0},{1,8},{2,16},{3,24},{4,32},{5,40},{6,48},{7,56},{8,1},{9,9},... | collective-permute-start | bytes 393224 | tf_op jit(solution)/shard_map/ppermute | solution.py:230
  107.8 2.2 %copy-start = (f32[8,2,512,128]{3,2,1,0:T(8,128)S(1)}, f32[8,2,512,128]{3,2,1,0:T(8,128)}, u32[]{:S(2)}) copy-start(f32[8,2,512,128]{3,2,1,0:T(8,128)} %all-gather.4.cloned.1.call-done.pieces_ref) | copy-start | bytes 12582916
  120.4 1.2 copy-start.4
Sparse Core Ops, SparseCore 0:
  9.4 63.1 all-gather.3
  85.3 35.0 all-gather.5

commit v2 on v1

--- a/solution.py
+++ b/solution.py
@@ -12,7 +12,7 @@
 SLICE = BLK // RANKS
 F32 = jnp.float32
 BF16 = jnp.bfloat16
-VMEM_LIMIT = 40 * 1024 * 1024
+VMEM_LIMIT = 56 * 1024 * 1024
 
 
 def vmem():
@@ -23,27 +23,45 @@
     return pl.BlockSpec(memory_space=pltpu.SMEM)
 
 
+def hbm():
+    return pl.BlockSpec(memory_space=pltpu.HBM)
+
+
 def params():
     return pltpu.CompilerParams(vmem_limit_bytes=VMEM_LIMIT)
 
 
-def top_rows_kernel(map_ref, front_ref, child_ref, out_ref, acc_ref):
+def top_rows_kernel(map_ref, front_hbm, child_hbm, out_ref, acc_ref, front_ref, child_ref, sems):
     leaf, row, col = (lax.axis_index(name) for name in ("leaf", "row", "col"))
     child = leaf // CHILD_SLOTS
-    hit = map_ref[child, (leaf % CHILD_SLOTS) * RANKS + row] == row
-
-    @pl.when(leaf == 0)
-    def _():
+    used = row < 2
+    hit = used & (map_ref[child, (leaf % CHILD_SLOTS) * RANKS + row] == row)
+    first = used & (leaf == 0)
+    front_copy = pltpu.make_async_copy(front_hbm, front_ref, sems.at[0])
+    child_copy = pltpu.make_async_copy(child_hbm, child_ref, sems.at[1])
+
+    @pl.when(first)
+    def _():
+        front_copy.start()
+
+    @pl.when(hit)
+    def _():
+        child_copy.start()
+
+    @pl.when(first)
+    def _():
+        front_copy.wait()
         for z in range(2):
             for j in range(SLOTS):
                 acc_ref[j, z] = front_ref[z, pl.ds(j, BLK, stride=SLOTS), :]
 
-    @pl.when(leaf != 0)
+    @pl.when(jnp.logical_not(first))
     def _():
         acc_ref[...] = jnp.zeros_like(acc_ref)
 
     @pl.when(hit)
     def _():
+        child_copy.wait()
         for k in range(CHILD_SLOTS):
             slot = map_ref[child, k * RANKS + col] // RANKS
             for z in range(2):
@@ -59,9 +77,14 @@
     return pl.pallas_call(
         top_rows_kernel,
         out_shape=jax.ShapeDtypeStruct((SLOTS, 2, BLK + SLICE, BLK), BF16),
-        in_specs=[smem(), vmem(), vmem()],
+        in_specs=[smem(), hbm(), hbm()],
         out_specs=vmem(),
-        scratch_shapes=[pltpu.VMEM((SLOTS, 2, BLK, BLK), F32)],
+        scratch_shapes=[
+            pltpu.VMEM((SLOTS, 2, BLK, BLK), F32),
+            pltpu.VMEM(front.shape, F32),
+            pltpu.VMEM(child.shape, F32),
+            pltpu.SemaphoreType.DMA((2,)),
+        ],
         compiler_params=params(),
         name="top_rows",
     )(child_map, front, child)
@@ -90,7 +113,7 @@
     return pl.pallas_call(
         assemble_kernel,
         out_shape=jax.ShapeDtypeStruct(front.shape, F32),
-        in_specs=[smem(), vmem(), pl.BlockSpec(memory_space=pl.ANY)],
+        in_specs=[smem(), vmem(), hbm()],
         out_specs=vmem(),
         scratch_shapes=[pltpu.VMEM(pieces.shape[1:], F32), pltpu.SemaphoreType.DMA],
         compiler_params=params(),
@@ -225,10 +248,10 @@
     pivot = spread(top[:, BLK:], "col")
     both = spread(jnp.concatenate([top[:, :BLK], pivot[0], pivot[1]], axis=1), "row")
     own = jnp.concatenate([both[0, :, :BLK], both[1, :, :BLK]], axis=1)
-    panel = lax.all_gather(own, "leaf", axis=0, tiled=False)
     swap = [(a * RANKS + b, b * RANKS + a) for a in range(RANKS) for b in range(RANKS)]
     rows = lax.ppermute(own, ("row", "col"), swap)
-    pivot_pieces = spread(both[:2, :, BLK:], "leaf")
+    pivot_pieces, own = lax.optimization_barrier((spread(both[:2, :, BLK:], "leaf"), own))
+    panel = spread(own, "leaf")
     left, mult = multipliers(pivot_pieces, rows)
     assembled = assemble(child_map, front, pieces)
     result = update(left, mult, panel.reshape(SLOTS, 4 * BLK, BLK), assembled)

time: 131 us -> 143 us (1.092)
  the two profiles are of different devices: /device:TPU:72 before, /device:TPU:65 now
where the time goes in v2:
time: 143 us; the launch traced here: 142 us
  blocking collectives  56 us (39%)
  waiting for transfers between devices  32.6 us (23%)
  starting transfers between devices  20.6 us (14%)
  Pallas kernels  15.4 us (11%)
  between operations  13.5 us (9%)
  local copies, waits for them, and re-layouts  4.31 us (3%)
    all_to_all x2, blocking collectives, exchange(): return lax.all_to_all(x, axis, 0, 0)  56 us
    all_to_all x3, waiting for transfers between devices, exchange(): return lax.all_to_all(x, axis, 0, 0)  25.1 us
    all_to_all x3, starting transfers between devices, exchange(): return lax.all_to_all(x, axis, 0, 0)  18.6 us
    ppermute x1, waiting for transfers between devices, local(): rows = lax.ppermute(own, ('row', 'col'), swap)  6.83 us
    pallas_call x1, Pallas kernels, assemble(): pl.pallas_call(assemble_kernel, out_shape=jax.ShapeDtypeStruct(front.shap...  4.81 us
    pallas_call x1, Pallas kernels, multipliers(): pl.pallas_call(multipliers_kernel, out_shape=(jax.ShapeDtypeStruct((width...  4.8 us
    pallas_call x1, Pallas kernels, top_rows(): pl.pallas_call(top_rows_kernel, out_shape=jax.ShapeDtypeStruct((SLOTS, 2,...  3.08 us
  transfers between devices with their start and end apart: 5, of which 4 were waited for; matrix products, arithmetic and copies ran while one was open for 2% of the time, Pallas kernels for 9%

profile of v2, /device:TPU:65, one launch (start us, length us, event | category | flops | bytes accessed | tf_op | source)
XLA Modules:
  0.0 142.4 jit_solution(12134448682341141210)
XLA Ops:
  6.5 0.0 all-gather.2.cloned.1.call-start
  6.5 0.7 all-gather.2.cloned.1.call-update
  7.3 3.1 %top_rows.1 = bf16[8,2,144,128]{3,2,1,0:T(8,128)(2,1)} custom-call(s32[2,32]{1,0:T(2,128)} %map_ref.3, f32[2,1024,128]{2,1,0:T(8,128)} %bitcast.16, f32[2,512,128]{2,1,0:T(8,128)} %bitcast.19), custom_call_target="tpu_custom_call" | custom-call | tf_op jit(solution)/shard_map/top_rows/pallas_call | solution.py:77
  10.3 24.0 %all_to_all.25 = bf16[8,2,144,128]{3,2,1,0:T(8,128)(2,1)S(1)} all-to-all(bf16[8,2,144,128]{3,2,1,0:T(8,128)(2,1)} %top_rows.1), channel_id=1, replica_groups=mesh['leaf'=8,'row'=8,'col'=8] {'leaf'}, dimensions={0} | all-to-all | bytes 1179648 | tf_op jit(solution)/shard_map/all_to_all | solution.py:235
  34.4 0.1 reduce_sum.12
  34.5 0.6 broadcast_in_dim.8
  35.1 11.7 %all-to-all-start.1 = ((bf16[8,2,16,128]{3,2,1,0:T(8,128)(2,1)}), bf16[8,2,16,128]{3,2,1,0:T(8,128)(2,1)S(1)}, u32[]{:S(2)}, u32[]{:S(2)}) async-start(bf16[8,2,16,128]{3,2,1,0:T(8,128)(2,1)} %broadcast_in_dim.8), calls=%async_computation.1 | async-start | bytes 131072 | tf_op jit(solution)/shard_map/all_to_all | solution.py:235
  46.8 4.6 %all-to-all-done.1 = bf16[8,2,16,128]{3,2,1,0:T(8,128)(2,1)S(1)} async-done(((bf16[8,2,16,128]{3,2,1,0:T(8,128)(2,1)}), bf16[8,2,16,128]{3,2,1,0:T(8,128)(2,1)S(1)}, u32[]{:S(2)}, u32[]{:S(2)}) %all-to-all-start.1) | async-done | bytes 65568 | tf_op jit(solution)/shard_map/all_to_all | solution.py:235
  51.4 0.1 broadcast_in_dim.9
  51.5 32.0 %all_to_all.26 = bf16[8,2,160,128]{3,2,1,0:T(8,128)(2,1)S(1)} all-to-all(bf16[8,2,160,128]{3,2,1,0:T(8,128)(2,1)S(1)} %broadcast_in_dim.9), channel_id=1, replica_groups=mesh['leaf'=8,'row'=8,'col'=8] {'row'}, dimensions={0} | all-to-all | bytes 1310720 | tf_op jit(solution)/shard_map/all_to_all | solution.py:235
  83.4 0.8 broadcast_in_dim.10
  84.2 3.4 %all-to-all-start.3 = ((bf16[8,2,2,32,128]{4,3,2,1,0:T(8,128)(2,1)}), bf16[8,2,2,32,128]{4,3,2,1,0:T(8,128)(2,1)S(1)}, u32[]{:S(2)}, u32[]{:S(2)}) async-start(bf16[8,2,2,32,128]{4,3,2,1,0:T(8,128)(2,1)} %broadcast_in_dim.10), calls=%async_computation.3 | async-start | bytes 524288 | tf_op jit(solution)/shard_map/all_to_all | solution.py:235
  87.7 10.4 %all-to-all-done.3.pieces_ref = bf16[8,2,2,32,128]{4,3,2,1,0:T(8,128)(2,1)S(1)} async-done(((bf16[8,2,2,32,128]{4,3,2,1,0:T(8,128)(2,1)}), bf16[8,2,2,32,128]{4,3,2,1,0:T(8,128)(2,1)S(1)}, u32[]{:S(2)}, u32[]{:S(2)}) %all-to-all-start.3) | async-done | bytes 262176 | tf_op jit(solution)/shard_map/all_to_all | solution.py:235
  98.1 0.0 copy-start.1
  98.1 1.2 broadcast_in_dim.11
  99.3 3.6 %all-to-all-start.4 = ((bf16[8,2,256,128]{3,2,1,0:T(8,128)(2,1)}), bf16[8,2,256,128]{3,2,1,0:T(8,128)(2,1)S(1)}, u32[]{:S(2)}, u32[]{:S(2)}) async-start(bf16[8,2,256,128]{3,2,1,0:T(8,128)(2,1)} %broadcast_in_dim.11), calls=%async_computation.4 | async-start | bytes 2097152 | tf_op jit(solution)/shard_map/all_to_all | solution.py:235
  102.8 1.9 %collective-permute-start = (bf16[2,256,128]{2,1,0:T(8,128)(2,1)S(1)}, bf16[2,256,128]{2,1,0:T(8,128)(2,1)S(1)}, u32[]{:S(2)}, u32[]{:S(2)}) collective-permute-start(bf16[2,256,128]{2,1,0:T(8,128)(2,1)S(1)} %pad_maximum_fusion), channel_id=1, source_target_pairs={{0,0},{1,8},{2,16},{3,24},{4,32},{5,40},{6,48},{7,56},{8,1},{9,9},... | collective-permute-start | bytes 393224 | tf_op jit(solution)/shard_map/ppermute | solution.py:252
  104.8 6.8 %collective-permute-done.rows_ref = bf16[2,256,128]{2,1,0:T(8,128)(2,1)S(1)} collective-permute-done((bf16[2,256,128]{2,1,0:T(8,128)(2,1)S(1)}, bf16[2,256,128]{2,1,0:T(8,128)(2,1)S(1)}, u32[]{:S(2)}, u32[]{:S(2)}) %collective-permute-start) | collective-permute-done | bytes 131104 | tf_op jit(solution)/shard_map/ppermute | solution.py:252
  111.6 0.0 copy-done.1
  111.6 0.0 copy-start.2
  111.6 0.7 copy-done.2
  112.3 4.8 %multipliers.1 = (bf16[256,512]{1,0:T(8,128)(2,1)}, f32[2,128,256]{2,1,0:T(8,128)}) custom-call(bf16[8,2,2,32,128]{4,3,2,1,0:T(8,128)(2,1)} %copy-done.1, bf16[2,256,128]{2,1,0:T(8,128)(2,1)} %copy-done.2), custom_call_target="tpu_custom_call" | custom-call | flops 3221225472 | bytes 1048576 | tf_op jit(solution)/shard_map/multipliers/pallas_call | solution.py:185
  117.1 0.0 all-gather.2.cloned.1.call-done.pieces_ref
  117.1 4.8 %assemble.1.front_ref = f32[2,1024,128]{2,1,0:T(8,128)} custom-call(s32[2,32]{1,0:T(2,128)} %map_ref.3, f32[2,1024,128]{2,1,0:T(8,128)} %bitcast.17, f32[8,2,512,128]{3,2,1,0:T(8,128)} %all-gather.2.cloned.1.call-done.pieces_ref), custom_call_target="tpu_custom_call" | custom-call | flops 1048576 | bytes 3145728 | tf_op jit(solution)/shard_map/assemble/pallas_call | solution.py:113
  121.9 10.0 %all-to-all-done.4 = bf16[8,2,256,128]{3,2,1,0:T(8,128)(2,1)S(1)} async-done(((bf16[8,2,256,128]{3,2,1,0:T(8,128)(2,1)}), bf16[8,2,256,128]{3,2,1,0:T(8,128)(2,1)S(1)}, u32[]{:S(2)}, u32[]{:S(2)}) %all-to-all-start.4) | async-done | bytes 1048608 | tf_op jit(solution)/shard_map/all_to_all | solution.py:235
  131.9 0.0 copy-start
  131.9 1.0 copy-done
  132.9 2.7 %update.1 = f32[2,1024,128]{2,1,0:T(8,128)} custom-call(bf16[256,512]{1,0:T(8,128)(2,1)} %get-tuple-element.10.left_ref, f32[2,128,256]{2,1,0:T(8,128)} %get-tuple-element.11.mult_ref, bf16[8,512,128]{2,1,0:T(8,128)(2,1)} %bitcast.15, f32[2,1024,128]{2,1,0:T(8,128)} %assemble.1.front_ref), custom_call_target="tpu_custom_call" | custom-call | tf_op jit(solution)/shard_map/update/pallas_call | solution.py:224
  (7 shorter events, 0.0 us)
Async XLA Ops:
  6.5 110.5 %all-gather.2.cloned.1.call-start = ((), (), s32[]{:S(2)}) async-start(), calls=%async_computation.5 | async-start | bytes 4718592 | tf_op jit(solution)/shard_map/all_gather | solution.py:245
  35.1 16.3 %all-to-all-start.1 = ((bf16[8,2,16,128]{3,2,1,0:T(8,128)(2,1)}), bf16[8,2,16,128]{3,2,1,0:T(8,128)(2,1)S(1)}, u32[]{:S(2)}, u32[]{:S(2)}) async-start(bf16[8,2,16,128]{3,2,1,0:T(8,128)(2,1)} %broadcast_in_dim.8), calls=%async_computation.1 | async-start | bytes 131072 | tf_op jit(solution)/shard_map/all_to_all | solution.py:235
  84.2 13.9 %all-to-all-start.3 = ((bf16[8,2,2,32,128]{4,3,2,1,0:T(8,128)(2,1)}), bf16[8,2,2,32,128]{4,3,2,1,0:T(8,128)(2,1)S(1)}, u32[]{:S(2)}, u32[]{:S(2)}) async-start(bf16[8,2,2,32,128]{4,3,2,1,0:T(8,128)(2,1)} %broadcast_in_dim.10), calls=%async_computation.3 | async-start | bytes 524288 | tf_op jit(solution)/shard_map/all_to_all | solution.py:235
  98.1 13.5 %copy-start.1 = (bf16[8,2,2,32,128]{4,3,2,1,0:T(8,128)(2,1)}, bf16[8,2,2,32,128]{4,3,2,1,0:T(8,128)(2,1)S(1)}, u32[]{:S(2)}) copy-start(bf16[8,2,2,32,128]{4,3,2,1,0:T(8,128)(2,1)S(1)} %all-to-all-done.3.pieces_ref) | copy-start | bytes 786436
  99.3 32.6 %all-to-all-start.4 = ((bf16[8,2,256,128]{3,2,1,0:T(8,128)(2,1)}), bf16[8,2,256,128]{3,2,1,0:T(8,128)(2,1)S(1)}, u32[]{:S(2)}, u32[]{:S(2)}) async-start(bf16[8,2,256,128]{3,2,1,0:T(8,128)(2,1)} %broadcast_in_dim.11), calls=%async_computation.4 | async-start | bytes 2097152 | tf_op jit(solution)/shard_map/all_to_all | solution.py:235
  102.8 8.8 %collective-permute-start = (bf16[2,256,128]{2,1,0:T(8,128)(2,1)S(1)}, bf16[2,256,128]{2,1,0:T(8,128)(2,1)S(1)}, u32[]{:S(2)}, u32[]{:S(2)}) collective-permute-start(bf16[2,256,128]{2,1,0:T(8,128)(2,1)S(1)} %pad_maximum_fusion), channel_id=1, source_target_pairs={{0,0},{1,8},{2,16},{3,24},{4,32},{5,40},{6,48},{7,56},{8,1},{9,9},... | collective-permute-start | bytes 393224 | tf_op jit(solution)/shard_map/ppermute | solution.py:252
  111.6 0.7 copy-start.2
  131.9 1.0 copy-start
Sparse Core Ops, SparseCore 0:
  9.4 63.9 all-gather.1

commit v3 on v2

--- a/solution.py
+++ b/solution.py
@@ -10,9 +10,15 @@
 CHILD_SLOTS = 4
 RANKS = 8
 SLICE = BLK // RANKS
+TAG = 16
+QUARTERS = 4
+QUARTER = BLK // QUARTERS
 F32 = jnp.float32
 BF16 = jnp.bfloat16
-VMEM_LIMIT = 56 * 1024 * 1024
+F16 = jnp.float16
+TOP = 13.0
+LARGE = 56 * 1024 * 1024
+SMALL = 24 * 1024 * 1024
 
 
 def vmem():
@@ -27,8 +33,8 @@
     return pl.BlockSpec(memory_space=pltpu.HBM)
 
 
-def params():
-    return pltpu.CompilerParams(vmem_limit_bytes=VMEM_LIMIT)
+def params(limit):
+    return pltpu.CompilerParams(vmem_limit_bytes=limit)
 
 
 def top_rows_kernel(map_ref, front_hbm, child_hbm, out_ref, acc_ref, front_ref, child_ref, sems):
@@ -85,38 +91,51 @@
             pltpu.VMEM(child.shape, F32),
             pltpu.SemaphoreType.DMA((2,)),
         ],
-        compiler_params=params(),
+        compiler_params=params(LARGE),
         name="top_rows",
     )(child_map, front, child)
 
 
-def assemble_kernel(map_ref, front_ref, pieces_ref, out_ref, piece_ref, sem):
-    leaf, row, col = (lax.axis_index(name) for name in ("leaf", "row", "col"))
+def route_kernel(map_ref, real_ref, imag_ref, out_ref):
+    leaf, row = lax.axis_index("leaf"), lax.axis_index("row")
+    child = leaf // CHILD_SLOTS
+    out_ref[...] = jnp.zeros_like(out_ref)
+    for k in range(CHILD_SLOTS):
+        target = map_ref[child, k * RANKS + row] // RANKS
+        for z, part_ref in enumerate((real_ref, imag_ref)):
+            out_ref[target, z] = part_ref[pl.ds(k, BLK, stride=CHILD_SLOTS), :].T
+
+
+def route(child_map, real_part, imag_part):
+    return pl.pallas_call(
+        route_kernel,
+        out_shape=jax.ShapeDtypeStruct((SLOTS, 2, BLK, BLK), F32),
+        in_specs=[smem(), vmem(), vmem()],
+        out_specs=vmem(),
+        compiler_params=params(SMALL),
+        cost_estimate=pl.CostEstimate(flops=1 << 20, bytes_accessed=2 << 20, transcendentals=0),
+        name="route",
+    )(child_map, real_part, imag_part)
+
+
+def assemble_kernel(map_ref, front_ref, pieces_ref, out_ref):
+    col = lax.axis_index("col")
     out_ref[...] = front_ref[...]
     for child in range(2):
-        for source in range(CHILD_SLOTS):
-            @pl.when(map_ref[child, source * RANKS + row] // RANKS == leaf)
-            def _():
-                copy = pltpu.make_async_copy(
-                    pieces_ref.at[child * CHILD_SLOTS + source], piece_ref, sem
-                )
-                copy.start()
-                copy.wait()
-                for k in range(CHILD_SLOTS):
-                    slot = map_ref[child, k * RANKS + col] // RANKS
-                    for z in range(2):
-                        where = pl.ds(slot, BLK, stride=SLOTS)
-                        out_ref[z, where, :] += piece_ref[z, pl.ds(k, BLK, stride=CHILD_SLOTS), :]
+        for k in range(CHILD_SLOTS):
+            slot = map_ref[child, k * RANKS + col] // RANKS
+            where = pl.ds(slot, BLK, stride=SLOTS)
+            for z in range(2):
+                out_ref[z, where, :] += pieces_ref[child * CHILD_SLOTS + k, z]
 
 
 def assemble(child_map, front, pieces):
     return pl.pallas_call(
         assemble_kernel,
         out_shape=jax.ShapeDtypeStruct(front.shape, F32),
-        in_specs=[smem(), vmem(), hbm()],
+        in_specs=[smem(), vmem(), vmem()],
         out_specs=vmem(),
-        scratch_shapes=[pltpu.VMEM(pieces.shape[1:], F32), pltpu.SemaphoreType.DMA],
-        compiler_params=params(),
+        compiler_params=params(SMALL),
         cost_estimate=pl.CostEstimate(flops=1 << 20, bytes_accessed=3 << 20, transcendentals=0),
         name="assemble",
     )(child_map, front, pieces)
@@ -144,15 +163,17 @@
     )
 
 
-def multipliers_kernel(pieces_ref, rows_ref, left_ref, mult_ref, a_ref):
+def multipliers_kernel(mine_ref, other_ref, same_ref, cross_ref, mult_ref, sent_ref, a_ref):
     width = 2 * BLK
+    left_here = lax.axis_index("col") % 2 == 0
     for d in range(RANKS):
         for h in range(2):
             for z in range(2):
-                for g in range(2):
-                    a_ref[
-                        z, h * BLK + d * SLICE : h * BLK + (d + 1) * SLICE, g * BLK : (g + 1) * BLK
-                    ] = pieces_ref[d, h, z, g * SLICE : (g + 1) * SLICE, :].astype(F32)
+                mine = mine_ref[d, z, h * SLICE : (h + 1) * SLICE, :].astype(F32)
+                other = other_ref[d, z, h * SLICE : (h + 1) * SLICE, :].astype(F32)
+                where = slice(h * BLK + d * SLICE, h * BLK + (d + 1) * SLICE)
+                a_ref[z, where, :BLK] = jnp.where(left_here, mine, other)
+                a_ref[z, where, BLK:] = jnp.where(left_here, other, mine)
     a_re, a_im = a_ref[0], a_ref[1]
     diagonal = lax.broadcasted_iota(jnp.int32, (width, width), 0) == lax.broadcasted_iota(
         jnp.int32, (width, width), 1
@@ -166,7 +187,16 @@
     e0 = (e_re, e_im)
     e1 = product(e0, e0)
     e2 = product(e1, e1)
-    r_re, r_im = rows_ref[0].astype(F32), rows_ref[1].astype(F32)
+    r_re, r_im = (
+        jnp.concatenate(
+            [
+                jnp.where(left_here, same_ref[z], cross_ref[z]),
+                jnp.where(left_here, cross_ref[z], same_ref[z]),
+            ],
+            axis=0,
+        ).astype(F32)
+        for z in range(2)
+    )
     t = (x_re * r_re - x_im * r_im, x_re * r_im + x_im * r_re)
     for e in (e0, e1, e2):
         step = product(e, t)
@@ -174,30 +204,30 @@
     w_re, w_im = t[0].T, t[1].T
     mult_ref[0] = w_re
     mult_ref[1] = w_im
-    left_ref[:BLK, :width] = w_re.astype(BF16)
-    left_ref[:BLK, width:] = (-w_im).astype(BF16)
-    left_ref[BLK:, :width] = w_im.astype(BF16)
-    left_ref[BLK:, width:] = w_re.astype(BF16)
-
-
-def multipliers(pieces, rows):
+    sent_ref[0] = w_re.astype(BF16)
+    sent_ref[1] = w_im.astype(BF16)
+
+
+def multipliers(mine, other, same, cross):
     width = 2 * BLK
     return pl.pallas_call(
         multipliers_kernel,
         out_shape=(
-            jax.ShapeDtypeStruct((width, 2 * width), BF16),
             jax.ShapeDtypeStruct((2, BLK, width), F32),
+            jax.ShapeDtypeStruct((2, BLK, width), BF16),
         ),
-        in_specs=[vmem(), vmem()],
+        in_specs=[vmem()] * 4,
         out_specs=(vmem(), vmem()),
         scratch_shapes=[pltpu.VMEM((2, width, width), F32)],
-        compiler_params=params(),
+        compiler_params=params(SMALL),
         cost_estimate=pl.CostEstimate(flops=3 << 30, bytes_accessed=1 << 20, transcendentals=0),
         name="multipliers",
-    )(pieces, rows)
-
-
-def update_kernel(left_ref, mult_ref, panel_ref, front_ref, out_ref):
+    )(mine, other, same, cross)
+
+
+def update_kernel(
+    w_ref, near_ref, far_ref, mult_ref, front_ref, q0_ref, q1_ref, q2_ref, q3_ref, out_ref, panel_ref
+):
     leaf, row, col = (lax.axis_index(name) for name in ("leaf", "row", "col"))
     is_pivot_row = (leaf == 0) & (row < 2)
 
@@ -207,7 +237,18 @@
 
     @pl.when(jnp.logical_not(is_pivot_row))
     def _():
-        left = left_ref[...]
+        w_re, w_im = (
+            jnp.where(col < 2, w_ref[z], jnp.where(col < 4, near_ref[z], far_ref[z])) for z in range(2)
+        )
+        left = jnp.concatenate(
+            [jnp.concatenate([w_re, -w_im], axis=1), jnp.concatenate([w_im, w_re], axis=1)], axis=0
+        )
+        for step, part_ref in enumerate((q0_ref, q1_ref, q2_ref, q3_ref)):
+            start = ((row % QUARTERS) ^ step) * QUARTER
+            for z in range(2):
+                for h in range(2):
+                    where = pl.ds(pl.multiple_of((z * 2 + h) * BLK + start, QUARTER), QUARTER)
+                    panel_ref[:, where, :] = part_ref[:, z, h * QUARTER : (h + 1) * QUARTER]
         for j in range(SLOTS):
             update = dot(left, panel_ref[j])
             where = pl.ds(j, BLK, stride=SLOTS)
@@ -220,15 +261,16 @@
                     out_ref[z, pl.ds(0, BLK, stride=SLOTS), :] = mult_ref[z, :, g * BLK : (g + 1) * BLK]
 
 
-def update(left, mult, panel, front):
+def update(w, near, far, mult, front, quarters):
     return pl.pallas_call(
         update_kernel,
         out_shape=jax.ShapeDtypeStruct(front.shape, F32),
-        in_specs=[vmem()] * 4,
+        in_specs=[vmem()] * 9,
         out_specs=vmem(),
-        compiler_params=params(),
+        scratch_shapes=[pltpu.VMEM((SLOTS, 4 * BLK, BLK), BF16)],
+        compiler_params=params(SMALL),
         name="update",
-    )(left, mult, panel, front)
+    )(w, near, far, mult, front, *quarters)
 
 
 def exchange(x, axis):
@@ -237,24 +279,79 @@
 
 def spread(x, axis):
     return exchange(jnp.broadcast_to(x[None], (RANKS,) + x.shape), axis)
+
+
+def shrink(child):
+    largest = jnp.max(jnp.abs(child))
+    exponent = jnp.clip(jnp.floor(jnp.log2(largest)), -100.0, 127.0)
+    values = (child * jnp.exp2(TOP - exponent)).astype(F16)
+    tag = jnp.broadcast_to(exponent.astype(F16), (TAG, BLK))
+    return jnp.concatenate([values[0], tag], axis=0), values[1]
 
 
 def local(parent_front, child_updates, child_map):
     front = parent_front.reshape(2, BLK * SLOTS, BLK)
     child = child_updates.reshape(2, BLK * CHILD_SLOTS, BLK)
-    pieces = lax.all_gather(child, "leaf", axis=0, tiled=False)
+    swap = [(a * RANKS + b, b * RANKS + a) for a in range(RANKS) for b in range(RANKS)]
+    real_part, imag_part = shrink(child)
+    real_part = lax.ppermute(real_part, ("row", "col"), swap)
     parts = exchange(top_rows(child_map, front, child), "leaf")
     top = jnp.sum(parts.astype(F32), axis=0).astype(BF16)
-    pivot = spread(top[:, BLK:], "col")
-    both = spread(jnp.concatenate([top[:, :BLK], pivot[0], pivot[1]], axis=1), "row")
-    own = jnp.concatenate([both[0, :, :BLK], both[1, :, :BLK]], axis=1)
-    swap = [(a * RANKS + b, b * RANKS + a) for a in range(RANKS) for b in range(RANKS)]
-    rows = lax.ppermute(own, ("row", "col"), swap)
-    pivot_pieces, own = lax.optimization_barrier((spread(both[:2, :, BLK:], "leaf"), own))
-    panel = spread(own, "leaf")
-    left, mult = multipliers(pivot_pieces, rows)
-    assembled = assemble(child_map, front, pieces)
-    result = update(left, mult, panel.reshape(SLOTS, 4 * BLK, BLK), assembled)
+    top, real_part = lax.optimization_barrier((top, real_part))
+    half, pivot = top[:, :BLK], top[:, BLK:]
+    parts = half.reshape(2, QUARTERS, QUARTER, BLK).transpose(1, 0, 2, 3)
+    parts = jnp.concatenate(
+        [
+            jnp.concatenate([parts, parts], axis=0),
+            jnp.broadcast_to(pivot[None], (RANKS,) + pivot.shape),
+        ],
+        axis=2,
+    )
+    both = exchange(parts, "row")
+    same = lax.ppermute(
+        half, ("row", "col"), [(h * RANKS + b, b * RANKS + h) for h in range(2) for b in range(RANKS)]
+    )
+    cross = lax.ppermute(
+        half,
+        ("row", "col"),
+        [(h * RANKS + b, b * RANKS + 1 - h) for h in range(2) for b in range(RANKS)],
+    )
+    both, same, cross = lax.optimization_barrier((both, same, cross))
+    imag_part = lax.ppermute(imag_part, ("row", "col"), swap)
+    got = spread(
+        jnp.concatenate(
+            [both[0, :, :QUARTER], both[1, :, :QUARTER], both[0, :, QUARTER:], both[1, :, QUARTER:]],
+            axis=1,
+        ),
+        "leaf",
+    )
+    body, tag = real_part[: SLOTS * BLK // 2], real_part[SLOTS * BLK // 2 :]
+    routed = route(child_map, body.astype(F32), imag_part.astype(F32))
+    routed = jnp.concatenate(
+        [
+            routed.reshape(SLOTS, 2 * BLK, BLK).astype(F16),
+            jnp.broadcast_to(tag[None], (SLOTS,) + tag.shape),
+        ],
+        axis=1,
+    )
+    _, routed = lax.optimization_barrier((got, routed))
+    pieces = exchange(routed, "leaf")
+    mine = got[:, :, 2 * QUARTER :]
+    other = lax.ppermute(mine, "col", [(0, 1), (1, 0)])
+    mult, w = multipliers(mine, other, same, cross)
+    quarters = [got[:, :, : 2 * QUARTER]]
+    for bit in (1, 2, 3):
+        step = [(a, a ^ bit) for a in range(RANKS)]
+        quarters.append(lax.ppermute(quarters[0], "row", step))
+    col = lax.axis_index("col")
+    near = lax.ppermute(w, "col", [(0, 2), (1, 3)])
+    far = lax.ppermute(
+        jnp.where(col < 2, w, near), "col", [(0, 4), (1, 5), (2, 6), (3, 7)]
+    )
+    scale = jnp.exp2(pieces[:, 2 * BLK, 0].astype(F32) - TOP)
+    pieces = pieces[:, : 2 * BLK].astype(F32) * scale[:, None, None]
+    assembled = assemble(child_map, front, pieces.reshape(SLOTS, 2, BLK, BLK))
+    result = update(w, near, far, mult, assembled, quarters)
     return result.reshape(parent_front.shape)
 
 

time: 143 us -> 106 us (0.74)
  the two profiles are of different devices: /device:TPU:65 before, /device:TPU:12 now
where the time goes in v3:
time: 106 us
  starting transfers between devices  63.9 us (60%)
  waiting for transfers between devices  27.2 us (26%)
  Pallas kernels  8.14 us (8%)
  other arithmetic  3.01 us (3%)
  local copies, waits for them, and re-layouts  2.29 us (2%)
  between operations  1.06 us (1%)
    all_to_all x4, starting transfers between devices, exchange(): return lax.all_to_all(x, axis, 0, 0)  32.9 us
    all_to_all x4, waiting for transfers between devices, exchange(): return lax.all_to_all(x, axis, 0, 0)  10.7 us
    ppermute x3, starting transfers between devices, local(): quarters.append(lax.ppermute(quarters[0], 'row', step))  9.95 us
    ppermute x1, starting transfers between devices, local(): imag_part = lax.ppermute(imag_part, ('row', 'col'), swap)  5.36 us
    ppermute x1, waiting for transfers between devices, local(): lax.ppermute(half, ('row', 'col'), [(h * RANKS + b, b * RANKS + 1 - h) fo...  5.28 us
    ppermute x1, starting transfers between devices, local(): real_part = lax.ppermute(real_part, ('row', 'col'), swap)  5.27 us
    ppermute x1, starting transfers between devices, local(): lax.ppermute(jnp.where(col < 2, w, near), 'col', [(0, 4), (1, 5), (2, 6),...  4.57 us
    ppermute x1, waiting for transfers between devices, local(): imag_part = lax.ppermute(imag_part, ('row', 'col'), swap)  4.04 us
  transfers between devices with their start and end apart: 14, of which 8 were waited for; matrix products, arithmetic and copies ran while one was open for 2% of the time, Pallas kernels for 4%

profile of v3, /device:TPU:12, one launch (start us, length us, event | category | flops | bytes accessed | tf_op | source)
XLA Modules:
  0.0 105.6 jit_solution(6463304519842662073)
XLA Ops:
  0.0 1.7 %top_rows.1 = bf16[8,2,144,128]{3,2,1,0:T(8,128)(2,1)} custom-call(s32[2,32]{1,0:T(2,128)} %map_ref.5, f32[2,1024,128]{2,1,0:T(8,128)} %bitcast.26, f32[2,512,128]{2,1,0:T(8,128)} %bitcast.28), custom_call_target="tpu_custom_call" | custom-call | tf_op jit(solution)/shard_map/top_rows/pallas_call | solution.py:83
  1.7 7.7 %all-to-all-start = ((bf16[8,2,144,128]{3,2,1,0:T(8,128)(2,1)}), bf16[8,2,144,128]{3,2,1,0:T(8,128)(2,1)S(1)}, u32[]{:S(2)}, u32[]{:S(2)}) async-start(bf16[8,2,144,128]{3,2,1,0:T(8,128)(2,1)} %top_rows.1), calls=%async_computation | async-start | bytes 1179648 | tf_op jit(solution)/shard_map/all_to_all | solution.py:277
  9.4 0.9 abs_reduce_fusion
  11.2 5.3 %collective-permute-start = (f16[528,128]{1,0:T(8,128)(2,1)S(1)}, f16[528,128]{1,0:T(8,128)(2,1)S(1)}, u32[]{:S(2)}, u32[]{:S(2)}) collective-permute-start(f16[528,128]{1,0:T(8,128)(2,1)S(1)} %concatenate.15), channel_id=1, source_target_pairs={{0,0},{1,8},{2,16},{3,24},{4,32},{5,40},{6,48},{7,56},{8,1},{9,9},... | collective-permute-start | bytes 405512 | tf_op jit(solution)/shard_map/ppermute | solution.py:297
  16.5 10.4 %all-to-all-done = bf16[8,2,144,128]{3,2,1,0:T(8,128)(2,1)S(1)} async-done(((bf16[8,2,144,128]{3,2,1,0:T(8,128)(2,1)}), bf16[8,2,144,128]{3,2,1,0:T(8,128)(2,1)S(1)}, u32[]{:S(2)}, u32[]{:S(2)}) %all-to-all-start) | async-done | bytes 589856 | tf_op jit(solution)/shard_map/all_to_all | solution.py:277
  27.0 0.7 pad_maximum_fusion.1
  27.7 13.2 %all-to-all-start.1 = ((bf16[8,2,48,128]{3,2,1,0:T(8,128)(2,1)}), bf16[8,2,48,128]{3,2,1,0:T(8,128)(2,1)S(1)}, u32[]{:S(2)}, u32[]{:S(2)}) async-start(bf16[8,2,48,128]{3,2,1,0:T(8,128)(2,1)} %pad_maximum_fusion.1), calls=%async_computation.1 | async-start | bytes 393216 | tf_op jit(solution)/shard_map/all_to_all | solution.py:277
  40.9 1.3 %collective-permute-start.2 = (bf16[2,128,128]{2,1,0:T(8,128)(2,1)S(1)}, bf16[2,128,128]{2,1,0:T(8,128)(2,1)S(1)}, u32[]{:S(2)}, u32[]{:S(2)}) collective-permute-start(bf16[2,128,128]{2,1,0:T(8,128)(2,1)S(1)} %slice.43), channel_id=1, source_target_pairs={{0,1},{1,9},{2,17},{3,25},{4,33},{5,41},{6,49},{7,57},{8,0},{9,8},... | collective-permute-start | bytes 196616 | tf_op jit(solution)/shard_map/ppermute | solution.py:314
  42.2 1.3 %collective-permute-start.1 = (bf16[2,128,128]{2,1,0:T(8,128)(2,1)S(1)}, bf16[2,128,128]{2,1,0:T(8,128)(2,1)S(1)}, u32[]{:S(2)}, u32[]{:S(2)}) collective-permute-start(bf16[2,128,128]{2,1,0:T(8,128)(2,1)S(1)} %slice.43), channel_id=1, source_target_pairs={{0,0},{1,8},{2,16},{3,24},{4,32},{5,40},{6,48},{7,56},{8,1},{9,9},... | collective-permute-start | bytes 196616 | tf_op jit(solution)/shard_map/ppermute | solution.py:311
  43.5 5.3 %collective-permute-done.2.cross_ref = bf16[2,128,128]{2,1,0:T(8,128)(2,1)S(1)} collective-permute-done((bf16[2,128,128]{2,1,0:T(8,128)(2,1)S(1)}, bf16[2,128,128]{2,1,0:T(8,128)(2,1)S(1)}, u32[]{:S(2)}, u32[]{:S(2)}) %collective-permute-start.2) | collective-permute-done | bytes 65568 | tf_op jit(solution)/shard_map/ppermute | solution.py:314
  48.8 2.0 %collective-permute-done.1.same_ref = bf16[2,128,128]{2,1,0:T(8,128)(2,1)S(1)} collective-permute-done((bf16[2,128,128]{2,1,0:T(8,128)(2,1)S(1)}, bf16[2,128,128]{2,1,0:T(8,128)(2,1)S(1)}, u32[]{:S(2)}, u32[]{:S(2)}) %collective-permute-start.1) | collective-permute-done | bytes 65568 | tf_op jit(solution)/shard_map/ppermute | solution.py:311
  50.8 0.8 broadcast_in_dim.7
  51.6 5.1 %all-to-all-start.2 = ((bf16[8,2,96,128]{3,2,1,0:T(8,128)(2,1)}), bf16[8,2,96,128]{3,2,1,0:T(8,128)(2,1)S(1)}, u32[]{:S(2)}, u32[]{:S(2)}) async-start(bf16[8,2,96,128]{3,2,1,0:T(8,128)(2,1)} %broadcast_in_dim.7), calls=%async_computation.2 | async-start | bytes 786432 | tf_op jit(solution)/shard_map/all_to_all | solution.py:277
  56.7 5.4 %collective-permute-start.6 = (f16[512,128]{1,0:T(8,128)(2,1)S(1)}, f16[512,128]{1,0:T(8,128)(2,1)S(1)}, u32[]{:S(2)}, u32[]{:S(2)}) collective-permute-start(f16[512,128]{1,0:T(8,128)(2,1)S(1)} %get-tuple-element.21), channel_id=1, source_target_pairs={{0,0},{1,8},{2,16},{3,24},{4,32},{5,40},{6,48},{7,56},{8,1},{9,9},... | collective-permute-start | bytes 393224 | tf_op jit(solution)/shard_map/ppermute | solution.py:320
  62.1 4.0 %collective-permute-done.6 = f16[512,128]{1,0:T(8,128)(2,1)S(1)} collective-permute-done((f16[512,128]{1,0:T(8,128)(2,1)S(1)}, f16[512,128]{1,0:T(8,128)(2,1)S(1)}, u32[]{:S(2)}, u32[]{:S(2)}) %collective-permute-start.6) | collective-permute-done | bytes 131104 | tf_op jit(solution)/shard_map/ppermute | solution.py:320
  66.2 0.6 copy-done.1
  66.8 0.7 route.1
  67.7 0.6 slice-done
  68.3 1.0 pad_maximum_fusion
  69.2 0.3 all-to-all-done.2
  69.5 6.9 %all-to-all-start.3 = ((f16[8,272,128]{2,1,0:T(8,128)(2,1)}), f16[8,272,128]{2,1,0:T(8,128)(2,1)S(1)}, u32[]{:S(2)}, u32[]{:S(2)}) async-start(f16[8,272,128]{2,1,0:T(8,128)(2,1)} %pad_maximum_fusion), calls=%async_computation.3 | async-start | bytes 1114112 | tf_op jit(solution)/shard_map/all_to_all | solution.py:277
  76.5 1.9 %collective-permute-start.3 = (bf16[8,2,32,128]{3,2,1,0:T(8,128)(2,1)S(1)}, bf16[8,2,32,128]{3,2,1,0:T(8,128)(2,1)S(1)}, u32[]{:S(2)}, u32[]{:S(2)}) collective-permute-start(bf16[8,2,32,128]{3,2,1,0:T(8,128)(2,1)S(1)} %slice.57.mine_ref), channel_id=1, source_target_pairs={{0,1},{1,0},{8,9},{9,8},{16,17},{17,16},{24,25},{25,24},{32,33},{3... | collective-permute-start | bytes 393224 | tf_op jit(solution)/shard_map/ppermute | solution.py:340
  78.4 1.3 %collective-permute-done.3.other_ref = bf16[8,2,32,128]{3,2,1,0:T(8,128)(2,1)S(1)} collective-permute-done((bf16[8,2,32,128]{3,2,1,0:T(8,128)(2,1)S(1)}, bf16[8,2,32,128]{3,2,1,0:T(8,128)(2,1)S(1)}, u32[]{:S(2)}, u32[]{:S(2)}) %collective-permute-start.3) | collective-permute-done | bytes 131104 | tf_op jit(solution)/shard_map/ppermute | solution.py:340
  79.7 3.0 %multipliers.1 = (f32[2,128,256]{2,1,0:T(8,128)S(1)}, bf16[2,128,256]{2,1,0:T(8,128)(2,1)S(1)}) custom-call(bf16[8,2,32,128]{3,2,1,0:T(8,128)(2,1)S(1)} %slice.57.mine_ref, bf16[8,2,32,128]{3,2,1,0:T(8,128)(2,1)S(1)} %collective-permute-done.3.other_ref, bf16[2,128,128]{2,1,0:T(8,128)(2,1)S(1)} %collective-permute-done.1.same_ref, ...), custom_call_target="tpu_custom_call" | custom-call | flops 3221225472 | bytes 1048576 | tf_op jit(solution)/shard_map/multipliers/pallas_call | solution.py:213
  82.7 1.3 %collective-permute-start.4 = (bf16[2,128,256]{2,1,0:T(8,128)(2,1)S(1)}, bf16[2,128,256]{2,1,0:T(8,128)(2,1)S(1)}, u32[]{:S(2)}, u32[]{:S(2)}) collective-permute-start(bf16[2,128,256]{2,1,0:T(8,128)(2,1)S(1)} %get-tuple-element.17.w_ref), channel_id=1, source_target_pairs={{0,2},{1,3},{8,10},{9,11},{16,18},{17,19},{24,26},{25,27},{32,34},... | collective-permute-start | bytes 393224 | tf_op jit(solution)/shard_map/ppermute | solution.py:347
  84.0 2.1 %collective-permute-start.9 = (bf16[8,2,64,128]{3,2,1,0:T(8,128)(2,1)S(1)}, bf16[8,2,64,128]{3,2,1,0:T(8,128)(2,1)S(1)}, u32[]{:S(2)}, u32[]{:S(2)}) collective-permute-start(bf16[8,2,64,128]{3,2,1,0:T(8,128)(2,1)S(1)} %slice.61.q0_ref), channel_id=1, source_target_pairs={{0,24},{8,16},{16,8},{24,0},{32,56},{40,48},{48,40},{56,32},{1,25}... | collective-permute-start | bytes 786440 | tf_op jit(solution)/shard_map/ppermute | solution.py:345
  86.1 4.4 %collective-permute-start.8 = (bf16[8,2,64,128]{3,2,1,0:T(8,128)(2,1)S(1)}, bf16[8,2,64,128]{3,2,1,0:T(8,128)(2,1)S(1)}, u32[]{:S(2)}, u32[]{:S(2)}) collective-permute-start(bf16[8,2,64,128]{3,2,1,0:T(8,128)(2,1)S(1)} %slice.61.q0_ref), channel_id=1, source_target_pairs={{0,16},{8,24},{16,0},{24,8},{32,48},{40,56},{48,32},{56,40},{1,17}... | collective-permute-start | bytes 786440 | tf_op jit(solution)/shard_map/ppermute | solution.py:345
  90.5 3.5 %collective-permute-start.7 = (bf16[8,2,64,128]{3,2,1,0:T(8,128)(2,1)S(1)}, bf16[8,2,64,128]{3,2,1,0:T(8,128)(2,1)S(1)}, u32[]{:S(2)}, u32[]{:S(2)}) collective-permute-start(bf16[8,2,64,128]{3,2,1,0:T(8,128)(2,1)S(1)} %slice.61.q0_ref), channel_id=1, source_target_pairs={{0,8},{8,0},{16,24},{24,16},{32,40},{40,32},{48,56},{56,48},{1,9},... | collective-permute-start | bytes 786440 | tf_op jit(solution)/shard_map/ppermute | solution.py:345
  94.1 4.6 %collective-permute-start.5 = (bf16[2,128,256]{2,1,0:T(8,128)(2,1)S(1)}, bf16[2,128,256]{2,1,0:T(8,128)(2,1)S(1)}, u32[]{:S(2)}, u32[]{:S(2)}) collective-permute-start(bf16[2,128,256]{2,1,0:T(8,128)(2,1)S(1)} %broadcast_select_fusion), channel_id=1, source_target_pairs={{0,4},{1,5},{2,6},{3,7},{8,12},{9,13},{10,14},{11,15},{16,20},{17,... | collective-permute-start | bytes 393224 | tf_op jit(solution)/shard_map/ppermute | solution.py:348
  98.9 1.0 assemble.1.front_ref
  100.1 3.7 %collective-permute-done.7.q1_ref = bf16[8,2,64,128]{3,2,1,0:T(8,128)(2,1)S(1)} collective-permute-done((bf16[8,2,64,128]{3,2,1,0:T(8,128)(2,1)S(1)}, bf16[8,2,64,128]{3,2,1,0:T(8,128)(2,1)S(1)}, u32[]{:S(2)}, u32[]{:S(2)}) %collective-permute-start.7) | collective-permute-done | bytes 262176 | tf_op jit(solution)/shard_map/ppermute | solution.py:345
  103.8 1.8 %update.1 = f32[2,1024,128]{2,1,0:T(8,128)} custom-call(bf16[2,128,256]{2,1,0:T(8,128)(2,1)S(1)} %get-tuple-element.17.w_ref, bf16[2,128,256]{2,1,0:T(8,128)(2,1)S(1)} %collective-permute-done.4.near_ref, bf16[2,128,256]{2,1,0:T(8,128)(2,1)S(1)} %collective-permute-done.5.far_ref, f32[2,128,256]{2,1,0:T(8,128)S(1)} %get-tuple-element.18.mult_ref, ...), custom_call_target="tpu_custom_call" | custom-call | tf_op jit(solution)/shard_map/update/pallas_call | solution.py:265
  (37 shorter events, 0.9 us)
Async XLA Ops:
  1.7 7.7 %copy-start.2 = (f32[2,1,128,4,128]{4,3,2,1,0:T(4,128)S(1)}, f32[2,1,128,4,128]{4,3,2,1,0:T(4,128)}, u32[]{:S(2)}) copy-start(f32[2,1,128,4,128]{4,3,2,1,0:T(4,128)} %param.4) | copy-start | bytes 1572868
  1.7 25.1 %all-to-all-start = ((bf16[8,2,144,128]{3,2,1,0:T(8,128)(2,1)}), bf16[8,2,144,128]{3,2,1,0:T(8,128)(2,1)S(1)}, u32[]{:S(2)}, u32[]{:S(2)}) async-start(bf16[8,2,144,128]{3,2,1,0:T(8,128)(2,1)} %top_rows.1), calls=%async_computation | async-start | bytes 1179648 | tf_op jit(solution)/shard_map/all_to_all | solution.py:277
  11.2 15.7 %collective-permute-start = (f16[528,128]{1,0:T(8,128)(2,1)S(1)}, f16[528,128]{1,0:T(8,128)(2,1)S(1)}, u32[]{:S(2)}, u32[]{:S(2)}) collective-permute-start(f16[528,128]{1,0:T(8,128)(2,1)S(1)} %concatenate.15), channel_id=1, source_target_pairs={{0,0},{1,8},{2,16},{3,24},{4,32},{5,40},{6,48},{7,56},{8,1},{9,9},... | collective-permute-start | bytes 405512 | tf_op jit(solution)/shard_map/ppermute | solution.py:297
  26.9 39.2 %copy-start.3 = (f16[528,128]{1,0:T(8,128)(2,1)}, f16[528,128]{1,0:T(8,128)(2,1)S(1)}, u32[]{:S(2)}) copy-start(f16[528,128]{1,0:T(8,128)(2,1)S(1)} %collective-permute-done) | copy-start | bytes 405508
  27.7 23.1 %all-to-all-start.1 = ((bf16[8,2,48,128]{3,2,1,0:T(8,128)(2,1)}), bf16[8,2,48,128]{3,2,1,0:T(8,128)(2,1)S(1)}, u32[]{:S(2)}, u32[]{:S(2)}) async-start(bf16[8,2,48,128]{3,2,1,0:T(8,128)(2,1)} %pad_maximum_fusion.1), calls=%async_computation.1 | async-start | bytes 393216 | tf_op jit(solution)/shard_map/all_to_all | solution.py:277
  40.9 7.9 %collective-permute-start.2 = (bf16[2,128,128]{2,1,0:T(8,128)(2,1)S(1)}, bf16[2,128,128]{2,1,0:T(8,128)(2,1)S(1)}, u32[]{:S(2)}, u32[]{:S(2)}) collective-permute-start(bf16[2,128,128]{2,1,0:T(8,128)(2,1)S(1)} %slice.43), channel_id=1, source_target_pairs={{0,1},{1,9},{2,17},{3,25},{4,33},{5,41},{6,49},{7,57},{8,0},{9,8},... | collective-permute-start | bytes 196616 | tf_op jit(solution)/shard_map/ppermute | solution.py:314
  42.2 8.6 %collective-permute-start.1 = (bf16[2,128,128]{2,1,0:T(8,128)(2,1)S(1)}, bf16[2,128,128]{2,1,0:T(8,128)(2,1)S(1)}, u32[]{:S(2)}, u32[]{:S(2)}) collective-permute-start(bf16[2,128,128]{2,1,0:T(8,128)(2,1)S(1)} %slice.43), channel_id=1, source_target_pairs={{0,0},{1,8},{2,16},{3,24},{4,32},{5,40},{6,48},{7,56},{8,1},{9,9},... | collective-permute-start | bytes 196616 | tf_op jit(solution)/shard_map/ppermute | solution.py:311
  51.6 17.9 %all-to-all-start.2 = ((bf16[8,2,96,128]{3,2,1,0:T(8,128)(2,1)}), bf16[8,2,96,128]{3,2,1,0:T(8,128)(2,1)S(1)}, u32[]{:S(2)}, u32[]{:S(2)}) async-start(bf16[8,2,96,128]{3,2,1,0:T(8,128)(2,1)} %broadcast_in_dim.7), calls=%async_computation.2 | async-start | bytes 786432 | tf_op jit(solution)/shard_map/all_to_all | solution.py:277
  56.7 9.4 %collective-permute-start.6 = (f16[512,128]{1,0:T(8,128)(2,1)S(1)}, f16[512,128]{1,0:T(8,128)(2,1)S(1)}, u32[]{:S(2)}, u32[]{:S(2)}) collective-permute-start(f16[512,128]{1,0:T(8,128)(2,1)S(1)} %get-tuple-element.21), channel_id=1, source_target_pairs={{0,0},{1,8},{2,16},{3,24},{4,32},{5,40},{6,48},{7,56},{8,1},{9,9},... | collective-permute-start | bytes 393224 | tf_op jit(solution)/shard_map/ppermute | solution.py:320
  66.1 0.7 copy-start.1
  67.6 0.7 slice-start
  69.5 29.1 %all-to-all-start.3 = ((f16[8,272,128]{2,1,0:T(8,128)(2,1)}), f16[8,272,128]{2,1,0:T(8,128)(2,1)S(1)}, u32[]{:S(2)}, u32[]{:S(2)}) async-start(f16[8,272,128]{2,1,0:T(8,128)(2,1)} %pad_maximum_fusion), calls=%async_computation.3 | async-start | bytes 1114112 | tf_op jit(solution)/shard_map/all_to_all | solution.py:277
  76.5 3.2 %collective-permute-start.3 = (bf16[8,2,32,128]{3,2,1,0:T(8,128)(2,1)S(1)}, bf16[8,2,32,128]{3,2,1,0:T(8,128)(2,1)S(1)}, u32[]{:S(2)}, u32[]{:S(2)}) collective-permute-start(bf16[8,2,32,128]{3,2,1,0:T(8,128)(2,1)S(1)} %slice.57.mine_ref), channel_id=1, source_target_pairs={{0,1},{1,0},{8,9},{9,8},{16,17},{17,16},{24,25},{25,24},{32,33},{3... | collective-permute-start | bytes 393224 | tf_op jit(solution)/shard_map/ppermute | solution.py:340
  82.7 11.3 %collective-permute-start.4 = (bf16[2,128,256]{2,1,0:T(8,128)(2,1)S(1)}, bf16[2,128,256]{2,1,0:T(8,128)(2,1)S(1)}, u32[]{:S(2)}, u32[]{:S(2)}) collective-permute-start(bf16[2,128,256]{2,1,0:T(8,128)(2,1)S(1)} %get-tuple-element.17.w_ref), channel_id=1, source_target_pairs={{0,2},{1,3},{8,10},{9,11},{16,18},{17,19},{24,26},{25,27},{32,34},... | collective-permute-start | bytes 393224 | tf_op jit(solution)/shard_map/ppermute | solution.py:347
  84.0 14.9 %copy-start = (f32[2,1,128,8,128]{4,3,2,1,0:T(8,128)S(1)}, f32[2,1,128,8,128]{4,3,2,1,0:T(8,128)}, u32[]{:S(2)}) copy-start(f32[2,1,128,8,128]{4,3,2,1,0:T(8,128)} %param.3) | copy-start | bytes 3145732
  84.0 16.0 %collective-permute-start.9 = (bf16[8,2,64,128]{3,2,1,0:T(8,128)(2,1)S(1)}, bf16[8,2,64,128]{3,2,1,0:T(8,128)(2,1)S(1)}, u32[]{:S(2)}, u32[]{:S(2)}) collective-permute-start(bf16[8,2,64,128]{3,2,1,0:T(8,128)(2,1)S(1)} %slice.61.q0_ref), channel_id=1, source_target_pairs={{0,24},{8,16},{16,8},{24,0},{32,56},{40,48},{48,40},{56,32},{1,25}... | collective-permute-start | bytes 786440 | tf_op jit(solution)/shard_map/ppermute | solution.py:345
  86.1 13.9 %collective-permute-start.8 = (bf16[8,2,64,128]{3,2,1,0:T(8,128)(2,1)S(1)}, bf16[8,2,64,128]{3,2,1,0:T(8,128)(2,1)S(1)}, u32[]{:S(2)}, u32[]{:S(2)}) collective-permute-start(bf16[8,2,64,128]{3,2,1,0:T(8,128)(2,1)S(1)} %slice.61.q0_ref), channel_id=1, source_target_pairs={{0,16},{8,24},{16,0},{24,8},{32,48},{40,56},{48,32},{56,40},{1,17}... | collective-permute-start | bytes 786440 | tf_op jit(solution)/shard_map/ppermute | solution.py:345
  90.5 13.3 %collective-permute-start.7 = (bf16[8,2,64,128]{3,2,1,0:T(8,128)(2,1)S(1)}, bf16[8,2,64,128]{3,2,1,0:T(8,128)(2,1)S(1)}, u32[]{:S(2)}, u32[]{:S(2)}) collective-permute-start(bf16[8,2,64,128]{3,2,1,0:T(8,128)(2,1)S(1)} %slice.61.q0_ref), channel_id=1, source_target_pairs={{0,8},{8,0},{16,24},{24,16},{32,40},{40,32},{48,56},{56,48},{1,9},... | collective-permute-start | bytes 786440 | tf_op jit(solution)/shard_map/ppermute | solution.py:345
  94.1 9.7 %collective-permute-start.5 = (bf16[2,128,256]{2,1,0:T(8,128)(2,1)S(1)}, bf16[2,128,256]{2,1,0:T(8,128)(2,1)S(1)}, u32[]{:S(2)}, u32[]{:S(2)}) collective-permute-start(bf16[2,128,256]{2,1,0:T(8,128)(2,1)S(1)} %broadcast_select_fusion), channel_id=1, source_target_pairs={{0,4},{1,5},{2,6},{3,7},{8,12},{9,13},{10,14},{11,15},{16,20},{17,... | collective-permute-start | bytes 393224 | tf_op jit(solution)/shard_map/ppermute | solution.py:348

commit v4 on v3

--- a/solution.py
+++ b/solution.py
@@ -40,19 +40,24 @@
 def top_rows_kernel(map_ref, front_hbm, child_hbm, out_ref, acc_ref, front_ref, child_ref, sems):
     leaf, row, col = (lax.axis_index(name) for name in ("leaf", "row", "col"))
     child = leaf // CHILD_SLOTS
-    used = row < 2
-    hit = used & (map_ref[child, (leaf % CHILD_SLOTS) * RANKS + row] == row)
-    first = used & (leaf == 0)
+    target = map_ref[child, (leaf % CHILD_SLOTS) * RANKS + row]
+    upright = (row >= 2) & (col < 2)
+    hit = (row < 2) & (target == row)
+    first = (row < 2) & (leaf == 0)
     front_copy = pltpu.make_async_copy(front_hbm, front_ref, sems.at[0])
     child_copy = pltpu.make_async_copy(child_hbm, child_ref, sems.at[1])
 
-    @pl.when(first)
+    @pl.when(first | upright)
     def _():
         front_copy.start()
 
-    @pl.when(hit)
+    @pl.when(hit | upright)
     def _():
         child_copy.start()
+
+    @pl.when(jnp.logical_not(first))
+    def _():
+        acc_ref[...] = jnp.zeros_like(acc_ref)
 
     @pl.when(first)
     def _():
@@ -61,10 +66,6 @@
             for j in range(SLOTS):
                 acc_ref[j, z] = front_ref[z, pl.ds(j, BLK, stride=SLOTS), :]
 
-    @pl.when(jnp.logical_not(first))
-    def _():
-        acc_ref[...] = jnp.zeros_like(acc_ref)
-
     @pl.when(hit)
     def _():
         child_copy.wait()
@@ -72,6 +73,18 @@
             slot = map_ref[child, k * RANKS + col] // RANKS
             for z in range(2):
                 acc_ref[slot, z] += child_ref[z, pl.ds(k, BLK, stride=CHILD_SLOTS), :]
+
+    @pl.when(upright)
+    def _():
+        front_copy.wait()
+        child_copy.wait()
+        for z in range(2):
+            acc_ref[leaf, z] = front_ref[z, pl.ds(0, BLK, stride=SLOTS), :].T
+        for k in range(CHILD_SLOTS):
+            @pl.when(map_ref[child, k * RANKS + col] < RANKS)
+            def _():
+                for z in range(2):
+                    acc_ref[target // RANKS, z] += child_ref[z, pl.ds(k, BLK, stride=CHILD_SLOTS), :].T
 
     for d in range(SLOTS):
         for z in range(2):
@@ -96,26 +109,30 @@
     )(child_map, front, child)
 
 
-def route_kernel(map_ref, real_ref, imag_ref, out_ref):
+def route_kernel(map_ref, real_ref, upper_ref, lower_ref, out_ref):
     leaf, row = lax.axis_index("leaf"), lax.axis_index("row")
     child = leaf // CHILD_SLOTS
     out_ref[...] = jnp.zeros_like(out_ref)
     for k in range(CHILD_SLOTS):
         target = map_ref[child, k * RANKS + row] // RANKS
-        for z, part_ref in enumerate((real_ref, imag_ref)):
-            out_ref[target, z] = part_ref[pl.ds(k, BLK, stride=CHILD_SLOTS), :].T
-
-
-def route(child_map, real_part, imag_part):
+        out_ref[target, :BLK, :] = real_ref[pl.ds(k, BLK, stride=CHILD_SLOTS), :].T
+        where = pl.ds(k, BLK // 2, stride=CHILD_SLOTS)
+        imag = jnp.concatenate([upper_ref[where, :], lower_ref[where, :]], axis=0)
+        out_ref[target, BLK : 2 * BLK, :] = imag.T
+    for d in range(SLOTS):
+        out_ref[d, 2 * BLK :, :] = real_ref[CHILD_SLOTS * BLK :, :]
+
+
+def route(child_map, real, upper, lower):
     return pl.pallas_call(
         route_kernel,
-        out_shape=jax.ShapeDtypeStruct((SLOTS, 2, BLK, BLK), F32),
-        in_specs=[smem(), vmem(), vmem()],
+        out_shape=jax.ShapeDtypeStruct((SLOTS, 2 * BLK + TAG, BLK), F32),
+        in_specs=[smem(), vmem(), vmem(), vmem()],
         out_specs=vmem(),
         compiler_params=params(SMALL),
         cost_estimate=pl.CostEstimate(flops=1 << 20, bytes_accessed=2 << 20, transcendentals=0),
         name="route",
-    )(child_map, real_part, imag_part)
+    )(child_map, real, upper, lower)
 
 
 def assemble_kernel(map_ref, front_ref, pieces_ref, out_ref):
@@ -150,20 +167,22 @@
     return jnp.dot(a, b, preferred_element_type=F32)
 
 
+def real_product(a, b):
+    return dot(a[0], b[0]) if len(a) == 1 else dot(a[0], b[0]) + (dot(a[0], b[1]) + dot(a[1], b[0]))
+
+
 def product(left, right):
-    ls = [split(x) for x in left]
-    rs = [split(x) for x in right]
-
-    def real(a, b):
-        return dot(a[0], b[0]) + (dot(a[0], b[1]) + dot(a[1], b[0]))
-
     return (
-        real(ls[0], rs[0]) - real(ls[1], rs[1]),
-        real(ls[0], rs[1]) + real(ls[1], rs[0]),
-    )
-
-
-def multipliers_kernel(mine_ref, other_ref, same_ref, cross_ref, mult_ref, sent_ref, a_ref):
+        real_product(left[0], right[0]) - real_product(left[1], right[1]),
+        real_product(left[0], right[1]) + real_product(left[1], right[0]),
+    )
+
+
+def rounded(pair):
+    return [(x.astype(BF16),) for x in pair]
+
+
+def multipliers_kernel(mine_ref, other_ref, half_ref, rest_ref, mult_ref, sent_ref, a_ref):
     width = 2 * BLK
     left_here = lax.axis_index("col") % 2 == 0
     for d in range(RANKS):
@@ -185,21 +204,24 @@
     e_re = jnp.where(diagonal, 0.0, -(x_re * a_re - x_im * a_im))
     e_im = jnp.where(diagonal, 0.0, -(x_re * a_im + x_im * a_re))
     e0 = (e_re, e_im)
-    e1 = product(e0, e0)
-    e2 = product(e1, e1)
+    e0_high = rounded(e0)
+    e1 = rounded(product(e0_high, e0_high))
+    e2 = rounded(product(e1, e1))
     r_re, r_im = (
         jnp.concatenate(
             [
-                jnp.where(left_here, same_ref[z], cross_ref[z]),
-                jnp.where(left_here, cross_ref[z], same_ref[z]),
+                jnp.where(left_here, half_ref[z], rest_ref[z]),
+                jnp.where(left_here, rest_ref[z], half_ref[z]),
             ],
             axis=0,
         ).astype(F32)
         for z in range(2)
     )
     t = (x_re * r_re - x_im * r_im, x_re * r_im + x_im * r_re)
-    for e in (e0, e1, e2):
-        step = product(e, t)
+    step = product([split(x) for x in e0], [split(x) for x in t])
+    t = (t[0] + step[0], t[1] + step[1])
+    for e in (e1, e2):
+        step = product(e, rounded(t))
         t = (t[0] + step[0], t[1] + step[1])
     w_re, w_im = t[0].T, t[1].T
     mult_ref[0] = w_re
@@ -208,7 +230,7 @@
     sent_ref[1] = w_im.astype(BF16)
 
 
-def multipliers(mine, other, same, cross):
+def multipliers(mine, other, half, rest):
     width = 2 * BLK
     return pl.pallas_call(
         multipliers_kernel,
@@ -222,7 +244,7 @@
         compiler_params=params(SMALL),
         cost_estimate=pl.CostEstimate(flops=3 << 30, bytes_accessed=1 << 20, transcendentals=0),
         name="multipliers",
-    )(mine, other, same, cross)
+    )(mine, other, half, rest)
 
 
 def update_kernel(
@@ -308,16 +330,14 @@
         axis=2,
     )
     both = exchange(parts, "row")
-    same = lax.ppermute(
-        half, ("row", "col"), [(h * RANKS + b, b * RANKS + h) for h in range(2) for b in range(RANKS)]
-    )
-    cross = lax.ppermute(
-        half,
-        ("row", "col"),
-        [(h * RANKS + b, b * RANKS + 1 - h) for h in range(2) for b in range(RANKS)],
-    )
-    both, same, cross = lax.optimization_barrier((both, same, cross))
-    imag_part = lax.ppermute(imag_part, ("row", "col"), swap)
+    row, col = lax.axis_index("row"), lax.axis_index("col")
+    corner = lax.ppermute(half, ("row", "col"), [(1, RANKS), (RANKS, 1)])
+    half = jnp.where((row < 2) & (row != col), corner, half)
+    rest = lax.ppermute(half, "col", [(0, 1), (1, 0)])
+    upper, lower = imag_part[: CHILD_SLOTS * BLK // 2], imag_part[CHILD_SLOTS * BLK // 2 :]
+    upper = lax.ppermute(upper, ("row", "col"), swap)
+    both, rest, upper = lax.optimization_barrier((both, rest, upper))
+    lower = lax.ppermute(lower, ("row", "col"), swap)
     got = spread(
         jnp.concatenate(
             [both[0, :, :QUARTER], both[1, :, :QUARTER], both[0, :, QUARTER:], both[1, :, QUARTER:]],
@@ -325,25 +345,16 @@
         ),
         "leaf",
     )
-    body, tag = real_part[: SLOTS * BLK // 2], real_part[SLOTS * BLK // 2 :]
-    routed = route(child_map, body.astype(F32), imag_part.astype(F32))
-    routed = jnp.concatenate(
-        [
-            routed.reshape(SLOTS, 2 * BLK, BLK).astype(F16),
-            jnp.broadcast_to(tag[None], (SLOTS,) + tag.shape),
-        ],
-        axis=1,
-    )
+    routed = route(child_map, real_part.astype(F32), upper.astype(F32), lower.astype(F32)).astype(F16)
     _, routed = lax.optimization_barrier((got, routed))
     pieces = exchange(routed, "leaf")
     mine = got[:, :, 2 * QUARTER :]
     other = lax.ppermute(mine, "col", [(0, 1), (1, 0)])
-    mult, w = multipliers(mine, other, same, cross)
+    mult, w = multipliers(mine, other, half, rest)
     quarters = [got[:, :, : 2 * QUARTER]]
     for bit in (1, 2, 3):
         step = [(a, a ^ bit) for a in range(RANKS)]
         quarters.append(lax.ppermute(quarters[0], "row", step))
-    col = lax.axis_index("col")
     near = lax.ppermute(w, "col", [(0, 2), (1, 3)])
     far = lax.ppermute(
         jnp.where(col < 2, w, near), "col", [(0, 4), (1, 5), (2, 6), (3, 7)]

time: 106 us -> 105 us (level)
  the two profiles are of different devices: /device:TPU:12 before, /device:TPU:8 now
where the time goes in v4:
time: 105 us; the launch traced here: 104 us
  starting transfers between devices  58.3 us (56%)
  waiting for transfers between devices  34.1 us (32%)
  Pallas kernels  6.99 us (7%)
  other arithmetic  2.93 us (3%)
    all_to_all x4, starting transfers between devices, exchange(): return lax.all_to_all(x, axis, 0, 0)  33.5 us
    all_to_all x4, waiting for transfers between devices, exchange(): return lax.all_to_all(x, axis, 0, 0)  27.1 us
    ppermute x3, starting transfers between devices, local(): quarters.append(lax.ppermute(quarters[0], 'row', step))  9.95 us
    ppermute x1, starting transfers between devices, local(): rest = lax.ppermute(half, 'col', [(0, 1), (1, 0)])  5.29 us
    ppermute x3, waiting for transfers between devices, local(): quarters.append(lax.ppermute(quarters[0], 'row', step))  4.8 us
    ppermute x1, starting transfers between devices, local(): lax.ppermute(jnp.where(col < 2, w, near), 'col', [(0, 4), (1, 5), (2, 6),...  3.25 us
  transfers between devices with their start and end apart: 15, of which 7 were waited for; matrix products, arithmetic and copies ran while one was open for 3% of the time, Pallas kernels for 3%

profile of v4, /device:TPU:8, one launch (start us, length us, event | category | flops | bytes accessed | tf_op | source)
XLA Modules:
  0.0 104.3 jit_solution(4625469255813635159)
XLA Ops:
  0.0 1.7 %top_rows.1 = bf16[8,2,144,128]{3,2,1,0:T(8,128)(2,1)} custom-call(s32[2,32]{1,0:T(2,128)} %map_ref.5, f32[2,1024,128]{2,1,0:T(8,128)} %bitcast.25, f32[2,512,128]{2,1,0:T(8,128)} %bitcast.27), custom_call_target="tpu_custom_call" | custom-call | tf_op jit(solution)/shard_map/top_rows/pallas_call | solution.py:96
  1.7 10.8 %all-to-all-start = ((bf16[8,2,144,128]{3,2,1,0:T(8,128)(2,1)}), bf16[8,2,144,128]{3,2,1,0:T(8,128)(2,1)S(1)}, u32[]{:S(2)}, u32[]{:S(2)}) async-start(bf16[8,2,144,128]{3,2,1,0:T(8,128)(2,1)} %top_rows.1), calls=%async_computation | async-start | bytes 1179648 | tf_op jit(solution)/shard_map/all_to_all | solution.py:299
  12.5 0.8 abs_reduce_fusion
  14.1 0.7 collective-permute-start
  14.8 13.1 %all-to-all-done = bf16[8,2,144,128]{3,2,1,0:T(8,128)(2,1)S(1)} async-done(((bf16[8,2,144,128]{3,2,1,0:T(8,128)(2,1)}), bf16[8,2,144,128]{3,2,1,0:T(8,128)(2,1)S(1)}, u32[]{:S(2)}, u32[]{:S(2)}) %all-to-all-start) | async-done | bytes 589856 | tf_op jit(solution)/shard_map/all_to_all | solution.py:299
  28.0 0.7 collective-permute-start.1
  28.7 0.7 pad_maximum_fusion
  29.4 13.1 %all-to-all-start.1 = ((bf16[8,2,48,128]{3,2,1,0:T(8,128)(2,1)}), bf16[8,2,48,128]{3,2,1,0:T(8,128)(2,1)S(1)}, u32[]{:S(2)}, u32[]{:S(2)}) async-start(bf16[8,2,48,128]{3,2,1,0:T(8,128)(2,1)} %pad_maximum_fusion), calls=%async_computation.1 | async-start | bytes 393216 | tf_op jit(solution)/shard_map/all_to_all | solution.py:299
  42.6 0.7 collective-permute-start.3
  43.3 5.3 %collective-permute-start.2 = (bf16[2,128,128]{2,1,0:T(8,128)(2,1)S(1)}, bf16[2,128,128]{2,1,0:T(8,128)(2,1)S(1)}, u32[]{:S(2)}, u32[]{:S(2)}) collective-permute-start(bf16[2,128,128]{2,1,0:T(8,128)(2,1)S(1)} %broadcast_select_fusion.1.half_ref), channel_id=1, source_target_pairs={{0,1},{1,0},{8,9},{9,8},{16,17},{17,16},{24,25},{25,24},{32,33},{3... | collective-permute-start | bytes 196616 | tf_op jit(solution)/shard_map/ppermute | solution.py:336
  48.6 0.9 collective-permute-done.2.rest_ref
  49.5 4.0 %all-to-all-done.1 = bf16[8,2,48,128]{3,2,1,0:T(8,128)(2,1)S(1)} async-done(((bf16[8,2,48,128]{3,2,1,0:T(8,128)(2,1)}), bf16[8,2,48,128]{3,2,1,0:T(8,128)(2,1)S(1)}, u32[]{:S(2)}, u32[]{:S(2)}) %all-to-all-start.1) | async-done | bytes 196640 | tf_op jit(solution)/shard_map/all_to_all | solution.py:299
  53.5 0.8 broadcast_in_dim.5
  54.3 4.7 %all-to-all-start.2 = ((bf16[8,2,96,128]{3,2,1,0:T(8,128)(2,1)}), bf16[8,2,96,128]{3,2,1,0:T(8,128)(2,1)S(1)}, u32[]{:S(2)}, u32[]{:S(2)}) async-start(bf16[8,2,96,128]{3,2,1,0:T(8,128)(2,1)} %broadcast_in_dim.5), calls=%async_computation.2 | async-start | bytes 786432 | tf_op jit(solution)/shard_map/all_to_all | solution.py:299
  59.0 0.7 collective-permute-start.7
  59.8 0.8 route.1
  60.5 0.9 convert_element_type.32
  61.4 10.0 %all-to-all-done.2 = bf16[8,2,96,128]{3,2,1,0:T(8,128)(2,1)S(1)} async-done(((bf16[8,2,96,128]{3,2,1,0:T(8,128)(2,1)}), bf16[8,2,96,128]{3,2,1,0:T(8,128)(2,1)S(1)}, u32[]{:S(2)}, u32[]{:S(2)}) %all-to-all-start.2) | async-done | bytes 393248 | tf_op jit(solution)/shard_map/all_to_all | solution.py:299
  71.4 4.9 %all-to-all-start.3 = ((f16[8,272,128]{2,1,0:T(8,128)(2,1)}), f16[8,272,128]{2,1,0:T(8,128)(2,1)S(1)}, u32[]{:S(2)}, u32[]{:S(2)}) async-start(f16[8,272,128]{2,1,0:T(8,128)(2,1)} %convert_element_type.32), calls=%async_computation.3 | async-start | bytes 1114112 | tf_op jit(solution)/shard_map/all_to_all | solution.py:299
  76.3 1.9 %collective-permute-start.4 = (bf16[8,2,32,128]{3,2,1,0:T(8,128)(2,1)S(1)}, bf16[8,2,32,128]{3,2,1,0:T(8,128)(2,1)S(1)}, u32[]{:S(2)}, u32[]{:S(2)}) collective-permute-start(bf16[8,2,32,128]{3,2,1,0:T(8,128)(2,1)S(1)} %slice.65.mine_ref), channel_id=1, source_target_pairs={{0,1},{1,0},{8,9},{9,8},{16,17},{17,16},{24,25},{25,24},{32,33},{3... | collective-permute-start | bytes 393224 | tf_op jit(solution)/shard_map/ppermute | solution.py:352
  78.2 1.3 %collective-permute-done.4.other_ref = bf16[8,2,32,128]{3,2,1,0:T(8,128)(2,1)S(1)} collective-permute-done((bf16[8,2,32,128]{3,2,1,0:T(8,128)(2,1)S(1)}, bf16[8,2,32,128]{3,2,1,0:T(8,128)(2,1)S(1)}, u32[]{:S(2)}, u32[]{:S(2)}) %collective-permute-start.4) | collective-permute-done | bytes 131104 | tf_op jit(solution)/shard_map/ppermute | solution.py:352
  79.5 1.8 %multipliers.1 = (f32[2,128,256]{2,1,0:T(8,128)S(1)}, bf16[2,128,256]{2,1,0:T(8,128)(2,1)S(1)}) custom-call(bf16[8,2,32,128]{3,2,1,0:T(8,128)(2,1)S(1)} %slice.65.mine_ref, bf16[8,2,32,128]{3,2,1,0:T(8,128)(2,1)S(1)} %collective-permute-done.4.other_ref, bf16[2,128,128]{2,1,0:T(8,128)(2,1)S(1)} %broadcast_select_fusion.1.half_ref, ...), custom_call_target="tpu_custom_call" | custom-call | flops 3221225472 | bytes 1048576 | tf_op jit(solution)/shard_map/multipliers/pallas_call | solution.py:235
  81.4 1.7 %collective-permute-start.5 = (bf16[2,128,256]{2,1,0:T(8,128)(2,1)S(1)}, bf16[2,128,256]{2,1,0:T(8,128)(2,1)S(1)}, u32[]{:S(2)}, u32[]{:S(2)}) collective-permute-start(bf16[2,128,256]{2,1,0:T(8,128)(2,1)S(1)} %get-tuple-element.16.w_ref), channel_id=1, source_target_pairs={{0,2},{1,3},{8,10},{9,11},{16,18},{17,19},{24,26},{25,27},{32,34},... | collective-permute-start | bytes 393224 | tf_op jit(solution)/shard_map/ppermute | solution.py:358
  83.1 3.9 %collective-permute-start.10 = (bf16[8,2,64,128]{3,2,1,0:T(8,128)(2,1)S(1)}, bf16[8,2,64,128]{3,2,1,0:T(8,128)(2,1)S(1)}, u32[]{:S(2)}, u32[]{:S(2)}) collective-permute-start(bf16[8,2,64,128]{3,2,1,0:T(8,128)(2,1)S(1)} %slice.69.q0_ref), channel_id=1, source_target_pairs={{0,24},{8,16},{16,8},{24,0},{32,56},{40,48},{48,40},{56,32},{1,25}... | collective-permute-start | bytes 786440 | tf_op jit(solution)/shard_map/ppermute | solution.py:357
  87.0 2.1 %collective-permute-start.9 = (bf16[8,2,64,128]{3,2,1,0:T(8,128)(2,1)S(1)}, bf16[8,2,64,128]{3,2,1,0:T(8,128)(2,1)S(1)}, u32[]{:S(2)}, u32[]{:S(2)}) collective-permute-start(bf16[8,2,64,128]{3,2,1,0:T(8,128)(2,1)S(1)} %slice.69.q0_ref), channel_id=1, source_target_pairs={{0,16},{8,24},{16,0},{24,8},{32,48},{40,56},{48,32},{56,40},{1,17}... | collective-permute-start | bytes 786440 | tf_op jit(solution)/shard_map/ppermute | solution.py:357
  89.1 4.0 %collective-permute-start.8 = (bf16[8,2,64,128]{3,2,1,0:T(8,128)(2,1)S(1)}, bf16[8,2,64,128]{3,2,1,0:T(8,128)(2,1)S(1)}, u32[]{:S(2)}, u32[]{:S(2)}) collective-permute-start(bf16[8,2,64,128]{3,2,1,0:T(8,128)(2,1)S(1)} %slice.69.q0_ref), channel_id=1, source_target_pairs={{0,8},{8,0},{16,24},{24,16},{32,40},{40,32},{48,56},{56,48},{1,9},... | collective-permute-start | bytes 786440 | tf_op jit(solution)/shard_map/ppermute | solution.py:357
  93.1 3.2 %collective-permute-start.6 = (bf16[2,128,256]{2,1,0:T(8,128)(2,1)S(1)}, bf16[2,128,256]{2,1,0:T(8,128)(2,1)S(1)}, u32[]{:S(2)}, u32[]{:S(2)}) collective-permute-start(bf16[2,128,256]{2,1,0:T(8,128)(2,1)S(1)} %broadcast_select_fusion), channel_id=1, source_target_pairs={{0,4},{1,5},{2,6},{3,7},{8,12},{9,13},{10,14},{11,15},{16,20},{17,... | collective-permute-start | bytes 393224 | tf_op jit(solution)/shard_map/ppermute | solution.py:359
  96.4 0.2 fusion.3
  96.7 1.0 assemble.1.front_ref
  97.7 2.3 %collective-permute-done.10.q3_ref = bf16[8,2,64,128]{3,2,1,0:T(8,128)(2,1)S(1)} collective-permute-done((bf16[8,2,64,128]{3,2,1,0:T(8,128)(2,1)S(1)}, bf16[8,2,64,128]{3,2,1,0:T(8,128)(2,1)S(1)}, u32[]{:S(2)}, u32[]{:S(2)}) %collective-permute-start.10) | collective-permute-done | bytes 262176 | tf_op jit(solution)/shard_map/ppermute | solution.py:357
  99.9 2.5 %collective-permute-done.8.q1_ref = bf16[8,2,64,128]{3,2,1,0:T(8,128)(2,1)S(1)} collective-permute-done((bf16[8,2,64,128]{3,2,1,0:T(8,128)(2,1)S(1)}, bf16[8,2,64,128]{3,2,1,0:T(8,128)(2,1)S(1)}, u32[]{:S(2)}, u32[]{:S(2)}) %collective-permute-start.8) | collective-permute-done | bytes 262176 | tf_op jit(solution)/shard_map/ppermute | solution.py:357
  102.5 1.8 %update.1 = f32[2,1024,128]{2,1,0:T(8,128)} custom-call(bf16[2,128,256]{2,1,0:T(8,128)(2,1)S(1)} %get-tuple-element.16.w_ref, bf16[2,128,256]{2,1,0:T(8,128)(2,1)S(1)} %collective-permute-done.5.near_ref, bf16[2,128,256]{2,1,0:T(8,128)(2,1)S(1)} %collective-permute-done.6.far_ref, f32[2,128,256]{2,1,0:T(8,128)S(1)} %get-tuple-element.17.mult_ref, ...), custom_call_target="tpu_custom_call" | custom-call | tf_op jit(solution)/shard_map/update/pallas_call | solution.py:287
  (34 shorter events, 0.6 us)
Async XLA Ops:
  1.7 10.8 %copy-start.2 = (f32[2,1,128,4,128]{4,3,2,1,0:T(4,128)S(1)}, f32[2,1,128,4,128]{4,3,2,1,0:T(4,128)}, u32[]{:S(2)}) copy-start(f32[2,1,128,4,128]{4,3,2,1,0:T(4,128)} %param.4) | copy-start | bytes 1572868
  1.7 26.2 %all-to-all-start = ((bf16[8,2,144,128]{3,2,1,0:T(8,128)(2,1)}), bf16[8,2,144,128]{3,2,1,0:T(8,128)(2,1)S(1)}, u32[]{:S(2)}, u32[]{:S(2)}) async-start(bf16[8,2,144,128]{3,2,1,0:T(8,128)(2,1)} %top_rows.1), calls=%async_computation | async-start | bytes 1179648 | tf_op jit(solution)/shard_map/all_to_all | solution.py:299
  14.1 13.8 %collective-permute-start = (f16[528,128]{1,0:T(8,128)(2,1)S(1)}, f16[528,128]{1,0:T(8,128)(2,1)S(1)}, u32[]{:S(2)}, u32[]{:S(2)}) collective-permute-start(f16[528,128]{1,0:T(8,128)(2,1)S(1)} %concatenate.12), channel_id=1, source_target_pairs={{0,0},{1,8},{2,16},{3,24},{4,32},{5,40},{6,48},{7,56},{8,1},{9,9},... | collective-permute-start | bytes 405512 | tf_op jit(solution)/shard_map/ppermute | solution.py:319
  28.0 15.3 %collective-permute-start.1 = (bf16[2,128,128]{2,1,0:T(8,128)(2,1)S(1)}, bf16[2,128,128]{2,1,0:T(8,128)(2,1)S(1)}, u32[]{:S(2)}, u32[]{:S(2)}) collective-permute-start(bf16[2,128,128]{2,1,0:T(8,128)(2,1)S(1)} %slice.49), channel_id=1, source_target_pairs={{1,8},{8,1},{65,72},{72,65},{129,136},{136,129},{193,200},{200,193... | collective-permute-start | bytes 196616 | tf_op jit(solution)/shard_map/ppermute | solution.py:334
  29.4 24.1 %all-to-all-start.1 = ((bf16[8,2,48,128]{3,2,1,0:T(8,128)(2,1)}), bf16[8,2,48,128]{3,2,1,0:T(8,128)(2,1)S(1)}, u32[]{:S(2)}, u32[]{:S(2)}) async-start(bf16[8,2,48,128]{3,2,1,0:T(8,128)(2,1)} %pad_maximum_fusion), calls=%async_computation.1 | async-start | bytes 393216 | tf_op jit(solution)/shard_map/all_to_all | solution.py:299
  42.6 6.0 %collective-permute-start.3 = (f16[256,128]{1,0:T(8,128)(2,1)S(1)}, f16[256,128]{1,0:T(8,128)(2,1)S(1)}, u32[]{:S(2)}, u32[]{:S(2)}) collective-permute-start(f16[256,128]{1,0:T(8,128)(2,1)S(1)} %get-tuple-element.22), channel_id=1, source_target_pairs={{0,0},{1,8},{2,16},{3,24},{4,32},{5,40},{6,48},{7,56},{8,1},{9,9},... | collective-permute-start | bytes 196616 | tf_op jit(solution)/shard_map/ppermute | solution.py:338
  43.3 16.5 %copy-start.1 = (s32[2,32]{1,0:T(2,128)S(1)}, s32[2,32]{1,0:T(2,128)}, u32[]{:S(2)}) copy-start(s32[2,32]{1,0:T(2,128)} %map_ref.5) | copy-start | bytes 772
  43.3 6.2 %collective-permute-start.2 = (bf16[2,128,128]{2,1,0:T(8,128)(2,1)S(1)}, bf16[2,128,128]{2,1,0:T(8,128)(2,1)S(1)}, u32[]{:S(2)}, u32[]{:S(2)}) collective-permute-start(bf16[2,128,128]{2,1,0:T(8,128)(2,1)S(1)} %broadcast_select_fusion.1.half_ref), channel_id=1, source_target_pairs={{0,1},{1,0},{8,9},{9,8},{16,17},{17,16},{24,25},{25,24},{32,33},{3... | collective-permute-start | bytes 196616 | tf_op jit(solution)/shard_map/ppermute | solution.py:336
  54.3 17.1 %all-to-all-start.2 = ((bf16[8,2,96,128]{3,2,1,0:T(8,128)(2,1)}), bf16[8,2,96,128]{3,2,1,0:T(8,128)(2,1)S(1)}, u32[]{:S(2)}, u32[]{:S(2)}) async-start(bf16[8,2,96,128]{3,2,1,0:T(8,128)(2,1)} %broadcast_in_dim.5), calls=%async_computation.2 | async-start | bytes 786432 | tf_op jit(solution)/shard_map/all_to_all | solution.py:299
  59.0 0.7 collective-permute-start.7
  71.4 25.0 %all-to-all-start.3 = ((f16[8,272,128]{2,1,0:T(8,128)(2,1)}), f16[8,272,128]{2,1,0:T(8,128)(2,1)S(1)}, u32[]{:S(2)}, u32[]{:S(2)}) async-start(f16[8,272,128]{2,1,0:T(8,128)(2,1)} %convert_element_type.32), calls=%async_computation.3 | async-start | bytes 1114112 | tf_op jit(solution)/shard_map/all_to_all | solution.py:299
  76.3 3.2 %collective-permute-start.4 = (bf16[8,2,32,128]{3,2,1,0:T(8,128)(2,1)S(1)}, bf16[8,2,32,128]{3,2,1,0:T(8,128)(2,1)S(1)}, u32[]{:S(2)}, u32[]{:S(2)}) collective-permute-start(bf16[8,2,32,128]{3,2,1,0:T(8,128)(2,1)S(1)} %slice.65.mine_ref), channel_id=1, source_target_pairs={{0,1},{1,0},{8,9},{9,8},{16,17},{17,16},{24,25},{25,24},{32,33},{3... | collective-permute-start | bytes 393224 | tf_op jit(solution)/shard_map/ppermute | solution.py:352
  81.4 11.7 %collective-permute-start.5 = (bf16[2,128,256]{2,1,0:T(8,128)(2,1)S(1)}, bf16[2,128,256]{2,1,0:T(8,128)(2,1)S(1)}, u32[]{:S(2)}, u32[]{:S(2)}) collective-permute-start(bf16[2,128,256]{2,1,0:T(8,128)(2,1)S(1)} %get-tuple-element.16.w_ref), channel_id=1, source_target_pairs={{0,2},{1,3},{8,10},{9,11},{16,18},{17,19},{24,26},{25,27},{32,34},... | collective-permute-start | bytes 393224 | tf_op jit(solution)/shard_map/ppermute | solution.py:358
  83.1 13.6 %copy-start = (f32[2,1,128,8,128]{4,3,2,1,0:T(8,128)S(1)}, f32[2,1,128,8,128]{4,3,2,1,0:T(8,128)}, u32[]{:S(2)}) copy-start(f32[2,1,128,8,128]{4,3,2,1,0:T(8,128)} %param.3) | copy-start | bytes 3145732
  83.1 16.8 %collective-permute-start.10 = (bf16[8,2,64,128]{3,2,1,0:T(8,128)(2,1)S(1)}, bf16[8,2,64,128]{3,2,1,0:T(8,128)(2,1)S(1)}, u32[]{:S(2)}, u32[]{:S(2)}) collective-permute-start(bf16[8,2,64,128]{3,2,1,0:T(8,128)(2,1)S(1)} %slice.69.q0_ref), channel_id=1, source_target_pairs={{0,24},{8,16},{16,8},{24,0},{32,56},{40,48},{48,40},{56,32},{1,25}... | collective-permute-start | bytes 786440 | tf_op jit(solution)/shard_map/ppermute | solution.py:357
  87.0 13.0 %collective-permute-start.9 = (bf16[8,2,64,128]{3,2,1,0:T(8,128)(2,1)S(1)}, bf16[8,2,64,128]{3,2,1,0:T(8,128)(2,1)S(1)}, u32[]{:S(2)}, u32[]{:S(2)}) collective-permute-start(bf16[8,2,64,128]{3,2,1,0:T(8,128)(2,1)S(1)} %slice.69.q0_ref), channel_id=1, source_target_pairs={{0,16},{8,24},{16,0},{24,8},{32,48},{40,56},{48,32},{56,40},{1,17}... | collective-permute-start | bytes 786440 | tf_op jit(solution)/shard_map/ppermute | solution.py:357
  89.1 13.4 %collective-permute-start.8 = (bf16[8,2,64,128]{3,2,1,0:T(8,128)(2,1)S(1)}, bf16[8,2,64,128]{3,2,1,0:T(8,128)(2,1)S(1)}, u32[]{:S(2)}, u32[]{:S(2)}) collective-permute-start(bf16[8,2,64,128]{3,2,1,0:T(8,128)(2,1)S(1)} %slice.69.q0_ref), channel_id=1, source_target_pairs={{0,8},{8,0},{16,24},{24,16},{32,40},{40,32},{48,56},{56,48},{1,9},... | collective-permute-start | bytes 786440 | tf_op jit(solution)/shard_map/ppermute | solution.py:357
  93.1 9.3 %collective-permute-start.6 = (bf16[2,128,256]{2,1,0:T(8,128)(2,1)S(1)}, bf16[2,128,256]{2,1,0:T(8,128)(2,1)S(1)}, u32[]{:S(2)}, u32[]{:S(2)}) collective-permute-start(bf16[2,128,256]{2,1,0:T(8,128)(2,1)S(1)} %broadcast_select_fusion), channel_id=1, source_target_pairs={{0,4},{1,5},{2,6},{3,7},{8,12},{9,13},{10,14},{11,15},{16,20},{17,... | collective-permute-start | bytes 393224 | tf_op jit(solution)/shard_map/ppermute | solution.py:359

commit v5 on v4

--- a/solution.py
+++ b/solution.py
@@ -266,7 +266,7 @@
             [jnp.concatenate([w_re, -w_im], axis=1), jnp.concatenate([w_im, w_re], axis=1)], axis=0
         )
         for step, part_ref in enumerate((q0_ref, q1_ref, q2_ref, q3_ref)):
-            start = ((row % QUARTERS) ^ step) * QUARTER
+            start = ((row % QUARTERS) ^ (0, 1, 3, 2)[step]) * QUARTER
             for z in range(2):
                 for h in range(2):
                     where = pl.ds(pl.multiple_of((z * 2 + h) * BLK + start, QUARTER), QUARTER)
@@ -352,7 +352,7 @@
     other = lax.ppermute(mine, "col", [(0, 1), (1, 0)])
     mult, w = multipliers(mine, other, half, rest)
     quarters = [got[:, :, : 2 * QUARTER]]
-    for bit in (1, 2, 3):
+    for bit in (1, 3, 2):
         step = [(a, a ^ bit) for a in range(RANKS)]
         quarters.append(lax.ppermute(quarters[0], "row", step))
     near = lax.ppermute(w, "col", [(0, 2), (1, 3)])

time: 105 us -> 103 us (0.981)
  waiting for transfers between devices: 34.1 us -> 32.3 us
    ppermute x3, waiting for transfers between devices: 4.8 us -> 3.04 us  [local(): quarters.append(lax.ppermute(quarters[0], 'row', step))]
  transfers between devices with their start and end apart: 15 -> 15, of which waited for: 7 -> 6; matrix products, arithmetic and copies ran while one was open for 3% -> 3% of each run, Pallas kernels for 3% -> 3%
where the time goes in v5:
time: 103 us; the launch traced here: 102 us
  starting transfers between devices  57.8 us (56%)
  waiting for transfers between devices  32.3 us (31%)
  Pallas kernels  7 us (7%)
  other arithmetic  2.93 us (3%)
    all_to_all x4, starting transfers between devices, exchange(): return lax.all_to_all(x, axis, 0, 0)  33.5 us
    all_to_all x4, waiting for transfers between devices, exchange(): return lax.all_to_all(x, axis, 0, 0)  27.1 us
    ppermute x3, starting transfers between devices, local(): quarters.append(lax.ppermute(quarters[0], 'row', step))  9.35 us
    ppermute x1, starting transfers between devices, local(): rest = lax.ppermute(half, 'col', [(0, 1), (1, 0)])  5.29 us
    ppermute x1, starting transfers between devices, local(): lax.ppermute(jnp.where(col < 2, w, near), 'col', [(0, 4), (1, 5), (2, 6),...  3.36 us
    ppermute x3, waiting for transfers between devices, local(): quarters.append(lax.ppermute(quarters[0], 'row', step))  3.04 us
  transfers between devices with their start and end apart: 15, of which 6 were waited for; matrix products, arithmetic and copies ran while one was open for 3% of the time, Pallas kernels for 3%

profile of v5, /device:TPU:8, one launch (start us, length us, event | category | flops | bytes accessed | tf_op | source)
XLA Modules:
  0.0 102.0 jit_solution(4025433723689967547)
XLA Ops:
  0.0 1.7 %top_rows.1 = bf16[8,2,144,128]{3,2,1,0:T(8,128)(2,1)} custom-call(s32[2,32]{1,0:T(2,128)} %map_ref.5, f32[2,1024,128]{2,1,0:T(8,128)} %bitcast.25, f32[2,512,128]{2,1,0:T(8,128)} %bitcast.27), custom_call_target="tpu_custom_call" | custom-call | tf_op jit(solution)/shard_map/top_rows/pallas_call | solution.py:96
  1.7 10.8 %all-to-all-start = ((bf16[8,2,144,128]{3,2,1,0:T(8,128)(2,1)}), bf16[8,2,144,128]{3,2,1,0:T(8,128)(2,1)S(1)}, u32[]{:S(2)}, u32[]{:S(2)}) async-start(bf16[8,2,144,128]{3,2,1,0:T(8,128)(2,1)} %top_rows.1), calls=%async_computation | async-start | bytes 1179648 | tf_op jit(solution)/shard_map/all_to_all | solution.py:299
  12.5 0.8 abs_reduce_fusion
  14.1 0.7 collective-permute-start
  14.8 13.1 %all-to-all-done = bf16[8,2,144,128]{3,2,1,0:T(8,128)(2,1)S(1)} async-done(((bf16[8,2,144,128]{3,2,1,0:T(8,128)(2,1)}), bf16[8,2,144,128]{3,2,1,0:T(8,128)(2,1)S(1)}, u32[]{:S(2)}, u32[]{:S(2)}) %all-to-all-start) | async-done | bytes 589856 | tf_op jit(solution)/shard_map/all_to_all | solution.py:299
  28.0 0.7 collective-permute-start.1
  28.7 0.7 pad_maximum_fusion
  29.4 13.1 %all-to-all-start.1 = ((bf16[8,2,48,128]{3,2,1,0:T(8,128)(2,1)}), bf16[8,2,48,128]{3,2,1,0:T(8,128)(2,1)S(1)}, u32[]{:S(2)}, u32[]{:S(2)}) async-start(bf16[8,2,48,128]{3,2,1,0:T(8,128)(2,1)} %pad_maximum_fusion), calls=%async_computation.1 | async-start | bytes 393216 | tf_op jit(solution)/shard_map/all_to_all | solution.py:299
  42.6 0.7 collective-permute-start.3
  43.3 5.3 %collective-permute-start.2 = (bf16[2,128,128]{2,1,0:T(8,128)(2,1)S(1)}, bf16[2,128,128]{2,1,0:T(8,128)(2,1)S(1)}, u32[]{:S(2)}, u32[]{:S(2)}) collective-permute-start(bf16[2,128,128]{2,1,0:T(8,128)(2,1)S(1)} %broadcast_select_fusion.1.half_ref), channel_id=1, source_target_pairs={{0,1},{1,0},{8,9},{9,8},{16,17},{17,16},{24,25},{25,24},{32,33},{3... | collective-permute-start | bytes 196616 | tf_op jit(solution)/shard_map/ppermute | solution.py:336
  48.6 0.9 collective-permute-done.2.rest_ref
  49.5 4.0 %all-to-all-done.1 = bf16[8,2,48,128]{3,2,1,0:T(8,128)(2,1)S(1)} async-done(((bf16[8,2,48,128]{3,2,1,0:T(8,128)(2,1)}), bf16[8,2,48,128]{3,2,1,0:T(8,128)(2,1)S(1)}, u32[]{:S(2)}, u32[]{:S(2)}) %all-to-all-start.1) | async-done | bytes 196640 | tf_op jit(solution)/shard_map/all_to_all | solution.py:299
  53.5 0.8 broadcast_in_dim.5
  54.3 4.7 %all-to-all-start.2 = ((bf16[8,2,96,128]{3,2,1,0:T(8,128)(2,1)}), bf16[8,2,96,128]{3,2,1,0:T(8,128)(2,1)S(1)}, u32[]{:S(2)}, u32[]{:S(2)}) async-start(bf16[8,2,96,128]{3,2,1,0:T(8,128)(2,1)} %broadcast_in_dim.5), calls=%async_computation.2 | async-start | bytes 786432 | tf_op jit(solution)/shard_map/all_to_all | solution.py:299
  59.0 0.7 collective-permute-start.7
  59.8 0.8 route.1
  60.5 0.9 convert_element_type.32
  61.4 10.0 %all-to-all-done.2 = bf16[8,2,96,128]{3,2,1,0:T(8,128)(2,1)S(1)} async-done(((bf16[8,2,96,128]{3,2,1,0:T(8,128)(2,1)}), bf16[8,2,96,128]{3,2,1,0:T(8,128)(2,1)S(1)}, u32[]{:S(2)}, u32[]{:S(2)}) %all-to-all-start.2) | async-done | bytes 393248 | tf_op jit(solution)/shard_map/all_to_all | solution.py:299
  71.4 4.9 %all-to-all-start.3 = ((f16[8,272,128]{2,1,0:T(8,128)(2,1)}), f16[8,272,128]{2,1,0:T(8,128)(2,1)S(1)}, u32[]{:S(2)}, u32[]{:S(2)}) async-start(f16[8,272,128]{2,1,0:T(8,128)(2,1)} %convert_element_type.32), calls=%async_computation.3 | async-start | bytes 1114112 | tf_op jit(solution)/shard_map/all_to_all | solution.py:299
  76.3 1.9 %collective-permute-start.4 = (bf16[8,2,32,128]{3,2,1,0:T(8,128)(2,1)S(1)}, bf16[8,2,32,128]{3,2,1,0:T(8,128)(2,1)S(1)}, u32[]{:S(2)}, u32[]{:S(2)}) collective-permute-start(bf16[8,2,32,128]{3,2,1,0:T(8,128)(2,1)S(1)} %slice.65.mine_ref), channel_id=1, source_target_pairs={{0,1},{1,0},{8,9},{9,8},{16,17},{17,16},{24,25},{25,24},{32,33},{3... | collective-permute-start | bytes 393224 | tf_op jit(solution)/shard_map/ppermute | solution.py:352
  78.2 1.3 %collective-permute-done.4.other_ref = bf16[8,2,32,128]{3,2,1,0:T(8,128)(2,1)S(1)} collective-permute-done((bf16[8,2,32,128]{3,2,1,0:T(8,128)(2,1)S(1)}, bf16[8,2,32,128]{3,2,1,0:T(8,128)(2,1)S(1)}, u32[]{:S(2)}, u32[]{:S(2)}) %collective-permute-start.4) | collective-permute-done | bytes 131104 | tf_op jit(solution)/shard_map/ppermute | solution.py:352
  79.5 1.8 %multipliers.1 = (f32[2,128,256]{2,1,0:T(8,128)S(1)}, bf16[2,128,256]{2,1,0:T(8,128)(2,1)S(1)}) custom-call(bf16[8,2,32,128]{3,2,1,0:T(8,128)(2,1)S(1)} %slice.65.mine_ref, bf16[8,2,32,128]{3,2,1,0:T(8,128)(2,1)S(1)} %collective-permute-done.4.other_ref, bf16[2,128,128]{2,1,0:T(8,128)(2,1)S(1)} %broadcast_select_fusion.1.half_ref, ...), custom_call_target="tpu_custom_call" | custom-call | flops 3221225472 | bytes 1048576 | tf_op jit(solution)/shard_map/multipliers/pallas_call | solution.py:235
  81.4 1.7 %collective-permute-start.5 = (bf16[2,128,256]{2,1,0:T(8,128)(2,1)S(1)}, bf16[2,128,256]{2,1,0:T(8,128)(2,1)S(1)}, u32[]{:S(2)}, u32[]{:S(2)}) collective-permute-start(bf16[2,128,256]{2,1,0:T(8,128)(2,1)S(1)} %get-tuple-element.16.w_ref), channel_id=1, source_target_pairs={{0,2},{1,3},{8,10},{9,11},{16,18},{17,19},{24,26},{25,27},{32,34},... | collective-permute-start | bytes 393224 | tf_op jit(solution)/shard_map/ppermute | solution.py:358
  83.1 3.3 %collective-permute-start.10 = (bf16[8,2,64,128]{3,2,1,0:T(8,128)(2,1)S(1)}, bf16[8,2,64,128]{3,2,1,0:T(8,128)(2,1)S(1)}, u32[]{:S(2)}, u32[]{:S(2)}) collective-permute-start(bf16[8,2,64,128]{3,2,1,0:T(8,128)(2,1)S(1)} %slice.69.q0_ref), channel_id=1, source_target_pairs={{0,16},{8,24},{16,0},{24,8},{32,48},{40,56},{48,32},{56,40},{1,17}... | collective-permute-start | bytes 786440 | tf_op jit(solution)/shard_map/ppermute | solution.py:357
  86.4 3.2 %collective-permute-start.9 = (bf16[8,2,64,128]{3,2,1,0:T(8,128)(2,1)S(1)}, bf16[8,2,64,128]{3,2,1,0:T(8,128)(2,1)S(1)}, u32[]{:S(2)}, u32[]{:S(2)}) collective-permute-start(bf16[8,2,64,128]{3,2,1,0:T(8,128)(2,1)S(1)} %slice.69.q0_ref), channel_id=1, source_target_pairs={{0,24},{8,16},{16,8},{24,0},{32,56},{40,48},{48,40},{56,32},{1,25}... | collective-permute-start | bytes 786440 | tf_op jit(solution)/shard_map/ppermute | solution.py:357
  89.7 2.8 %collective-permute-start.8 = (bf16[8,2,64,128]{3,2,1,0:T(8,128)(2,1)S(1)}, bf16[8,2,64,128]{3,2,1,0:T(8,128)(2,1)S(1)}, u32[]{:S(2)}, u32[]{:S(2)}) collective-permute-start(bf16[8,2,64,128]{3,2,1,0:T(8,128)(2,1)S(1)} %slice.69.q0_ref), channel_id=1, source_target_pairs={{0,8},{8,0},{16,24},{24,16},{32,40},{40,32},{48,56},{56,48},{1,9},... | collective-permute-start | bytes 786440 | tf_op jit(solution)/shard_map/ppermute | solution.py:357
  92.5 3.4 %collective-permute-start.6 = (bf16[2,128,256]{2,1,0:T(8,128)(2,1)S(1)}, bf16[2,128,256]{2,1,0:T(8,128)(2,1)S(1)}, u32[]{:S(2)}, u32[]{:S(2)}) collective-permute-start(bf16[2,128,256]{2,1,0:T(8,128)(2,1)S(1)} %broadcast_select_fusion), channel_id=1, source_target_pairs={{0,4},{1,5},{2,6},{3,7},{8,12},{9,13},{10,14},{11,15},{16,20},{17,... | collective-permute-start | bytes 393224 | tf_op jit(solution)/shard_map/ppermute | solution.py:359
  95.9 0.2 fusion.3
  96.1 0.1 convert_multiply_fusion
  96.2 1.0 assemble.1.front_ref
  97.2 3.0 %collective-permute-done.9.q2_ref = bf16[8,2,64,128]{3,2,1,0:T(8,128)(2,1)S(1)} collective-permute-done((bf16[8,2,64,128]{3,2,1,0:T(8,128)(2,1)S(1)}, bf16[8,2,64,128]{3,2,1,0:T(8,128)(2,1)S(1)}, u32[]{:S(2)}, u32[]{:S(2)}) %collective-permute-start.9) | collective-permute-done | bytes 262176 | tf_op jit(solution)/shard_map/ppermute | solution.py:357
  100.2 1.8 %update.1 = f32[2,1024,128]{2,1,0:T(8,128)} custom-call(bf16[2,128,256]{2,1,0:T(8,128)(2,1)S(1)} %get-tuple-element.16.w_ref, bf16[2,128,256]{2,1,0:T(8,128)(2,1)S(1)} %collective-permute-done.5.near_ref, bf16[2,128,256]{2,1,0:T(8,128)(2,1)S(1)} %collective-permute-done.6.far_ref, f32[2,128,256]{2,1,0:T(8,128)S(1)} %get-tuple-element.17.mult_ref, ...), custom_call_target="tpu_custom_call" | custom-call | tf_op jit(solution)/shard_map/update/pallas_call | solution.py:287
  (34 shorter events, 0.4 us)
Async XLA Ops:
  1.7 10.8 %copy-start.2 = (f32[2,1,128,4,128]{4,3,2,1,0:T(4,128)S(1)}, f32[2,1,128,4,128]{4,3,2,1,0:T(4,128)}, u32[]{:S(2)}) copy-start(f32[2,1,128,4,128]{4,3,2,1,0:T(4,128)} %param.4) | copy-start | bytes 1572868
  1.7 26.2 %all-to-all-start = ((bf16[8,2,144,128]{3,2,1,0:T(8,128)(2,1)}), bf16[8,2,144,128]{3,2,1,0:T(8,128)(2,1)S(1)}, u32[]{:S(2)}, u32[]{:S(2)}) async-start(bf16[8,2,144,128]{3,2,1,0:T(8,128)(2,1)} %top_rows.1), calls=%async_computation | async-start | bytes 1179648 | tf_op jit(solution)/shard_map/all_to_all | solution.py:299
  14.1 13.8 %collective-permute-start = (f16[528,128]{1,0:T(8,128)(2,1)S(1)}, f16[528,128]{1,0:T(8,128)(2,1)S(1)}, u32[]{:S(2)}, u32[]{:S(2)}) collective-permute-start(f16[528,128]{1,0:T(8,128)(2,1)S(1)} %concatenate.12), channel_id=1, source_target_pairs={{0,0},{1,8},{2,16},{3,24},{4,32},{5,40},{6,48},{7,56},{8,1},{9,9},... | collective-permute-start | bytes 405512 | tf_op jit(solution)/shard_map/ppermute | solution.py:319
  28.0 15.3 %collective-permute-start.1 = (bf16[2,128,128]{2,1,0:T(8,128)(2,1)S(1)}, bf16[2,128,128]{2,1,0:T(8,128)(2,1)S(1)}, u32[]{:S(2)}, u32[]{:S(2)}) collective-permute-start(bf16[2,128,128]{2,1,0:T(8,128)(2,1)S(1)} %slice.49), channel_id=1, source_target_pairs={{1,8},{8,1},{65,72},{72,65},{129,136},{136,129},{193,200},{200,193... | collective-permute-start | bytes 196616 | tf_op jit(solution)/shard_map/ppermute | solution.py:334
  29.4 24.1 %all-to-all-start.1 = ((bf16[8,2,48,128]{3,2,1,0:T(8,128)(2,1)}), bf16[8,2,48,128]{3,2,1,0:T(8,128)(2,1)S(1)}, u32[]{:S(2)}, u32[]{:S(2)}) async-start(bf16[8,2,48,128]{3,2,1,0:T(8,128)(2,1)} %pad_maximum_fusion), calls=%async_computation.1 | async-start | bytes 393216 | tf_op jit(solution)/shard_map/all_to_all | solution.py:299
  42.6 6.0 %collective-permute-start.3 = (f16[256,128]{1,0:T(8,128)(2,1)S(1)}, f16[256,128]{1,0:T(8,128)(2,1)S(1)}, u32[]{:S(2)}, u32[]{:S(2)}) collective-permute-start(f16[256,128]{1,0:T(8,128)(2,1)S(1)} %get-tuple-element.22), channel_id=1, source_target_pairs={{0,0},{1,8},{2,16},{3,24},{4,32},{5,40},{6,48},{7,56},{8,1},{9,9},... | collective-permute-start | bytes 196616 | tf_op jit(solution)/shard_map/ppermute | solution.py:338
  43.3 16.5 %copy-start.1 = (s32[2,32]{1,0:T(2,128)S(1)}, s32[2,32]{1,0:T(2,128)}, u32[]{:S(2)}) copy-start(s32[2,32]{1,0:T(2,128)} %map_ref.5) | copy-start | bytes 772
  43.3 6.2 %collective-permute-start.2 = (bf16[2,128,128]{2,1,0:T(8,128)(2,1)S(1)}, bf16[2,128,128]{2,1,0:T(8,128)(2,1)S(1)}, u32[]{:S(2)}, u32[]{:S(2)}) collective-permute-start(bf16[2,128,128]{2,1,0:T(8,128)(2,1)S(1)} %broadcast_select_fusion.1.half_ref), channel_id=1, source_target_pairs={{0,1},{1,0},{8,9},{9,8},{16,17},{17,16},{24,25},{25,24},{32,33},{3... | collective-permute-start | bytes 196616 | tf_op jit(solution)/shard_map/ppermute | solution.py:336
  54.3 17.1 %all-to-all-start.2 = ((bf16[8,2,96,128]{3,2,1,0:T(8,128)(2,1)}), bf16[8,2,96,128]{3,2,1,0:T(8,128)(2,1)S(1)}, u32[]{:S(2)}, u32[]{:S(2)}) async-start(bf16[8,2,96,128]{3,2,1,0:T(8,128)(2,1)} %broadcast_in_dim.5), calls=%async_computation.2 | async-start | bytes 786432 | tf_op jit(solution)/shard_map/all_to_all | solution.py:299
  59.0 0.7 collective-permute-start.7
  71.4 24.5 %all-to-all-start.3 = ((f16[8,272,128]{2,1,0:T(8,128)(2,1)}), f16[8,272,128]{2,1,0:T(8,128)(2,1)S(1)}, u32[]{:S(2)}, u32[]{:S(2)}) async-start(f16[8,272,128]{2,1,0:T(8,128)(2,1)} %convert_element_type.32), calls=%async_computation.3 | async-start | bytes 1114112 | tf_op jit(solution)/shard_map/all_to_all | solution.py:299
  76.3 3.2 %collective-permute-start.4 = (bf16[8,2,32,128]{3,2,1,0:T(8,128)(2,1)S(1)}, bf16[8,2,32,128]{3,2,1,0:T(8,128)(2,1)S(1)}, u32[]{:S(2)}, u32[]{:S(2)}) collective-permute-start(bf16[8,2,32,128]{3,2,1,0:T(8,128)(2,1)S(1)} %slice.65.mine_ref), channel_id=1, source_target_pairs={{0,1},{1,0},{8,9},{9,8},{16,17},{17,16},{24,25},{25,24},{32,33},{3... | collective-permute-start | bytes 393224 | tf_op jit(solution)/shard_map/ppermute | solution.py:352
  81.4 11.1 %collective-permute-start.5 = (bf16[2,128,256]{2,1,0:T(8,128)(2,1)S(1)}, bf16[2,128,256]{2,1,0:T(8,128)(2,1)S(1)}, u32[]{:S(2)}, u32[]{:S(2)}) collective-permute-start(bf16[2,128,256]{2,1,0:T(8,128)(2,1)S(1)} %get-tuple-element.16.w_ref), channel_id=1, source_target_pairs={{0,2},{1,3},{8,10},{9,11},{16,18},{17,19},{24,26},{25,27},{32,34},... | collective-permute-start | bytes 393224 | tf_op jit(solution)/shard_map/ppermute | solution.py:358
  83.1 13.1 %copy-start = (f32[2,1,128,8,128]{4,3,2,1,0:T(8,128)S(1)}, f32[2,1,128,8,128]{4,3,2,1,0:T(8,128)}, u32[]{:S(2)}) copy-start(f32[2,1,128,8,128]{4,3,2,1,0:T(8,128)} %param.3) | copy-start | bytes 3145732
  83.1 14.1 %collective-permute-start.10 = (bf16[8,2,64,128]{3,2,1,0:T(8,128)(2,1)S(1)}, bf16[8,2,64,128]{3,2,1,0:T(8,128)(2,1)S(1)}, u32[]{:S(2)}, u32[]{:S(2)}) collective-permute-start(bf16[8,2,64,128]{3,2,1,0:T(8,128)(2,1)S(1)} %slice.69.q0_ref), channel_id=1, source_target_pairs={{0,16},{8,24},{16,0},{24,8},{32,48},{40,56},{48,32},{56,40},{1,17}... | collective-permute-start | bytes 786440 | tf_op jit(solution)/shard_map/ppermute | solution.py:357
  86.4 13.8 %collective-permute-start.9 = (bf16[8,2,64,128]{3,2,1,0:T(8,128)(2,1)S(1)}, bf16[8,2,64,128]{3,2,1,0:T(8,128)(2,1)S(1)}, u32[]{:S(2)}, u32[]{:S(2)}) collective-permute-start(bf16[8,2,64,128]{3,2,1,0:T(8,128)(2,1)S(1)} %slice.69.q0_ref), channel_id=1, source_target_pairs={{0,24},{8,16},{16,8},{24,0},{32,56},{40,48},{48,40},{56,32},{1,25}... | collective-permute-start | bytes 786440 | tf_op jit(solution)/shard_map/ppermute | solution.py:357
  89.7 10.5 %collective-permute-start.8 = (bf16[8,2,64,128]{3,2,1,0:T(8,128)(2,1)S(1)}, bf16[8,2,64,128]{3,2,1,0:T(8,128)(2,1)S(1)}, u32[]{:S(2)}, u32[]{:S(2)}) collective-permute-start(bf16[8,2,64,128]{3,2,1,0:T(8,128)(2,1)S(1)} %slice.69.q0_ref), channel_id=1, source_target_pairs={{0,8},{8,0},{16,24},{24,16},{32,40},{40,32},{48,56},{56,48},{1,9},... | collective-permute-start | bytes 786440 | tf_op jit(solution)/shard_map/ppermute | solution.py:357
  92.5 7.7 %collective-permute-start.6 = (bf16[2,128,256]{2,1,0:T(8,128)(2,1)S(1)}, bf16[2,128,256]{2,1,0:T(8,128)(2,1)S(1)}, u32[]{:S(2)}, u32[]{:S(2)}) collective-permute-start(bf16[2,128,256]{2,1,0:T(8,128)(2,1)S(1)} %broadcast_select_fusion), channel_id=1, source_target_pairs={{0,4},{1,5},{2,6},{3,7},{8,12},{9,13},{10,14},{11,15},{16,20},{17,... | collective-permute-start | bytes 393224 | tf_op jit(solution)/shard_map/ppermute | solution.py:359
